TPU v7x, 32 devices: a whole 2x2x4 slice. The times are simulated.
32 devices in a mesh: dp: 2 (over core), vocab: 16 (over z, y, x).
Axes of the slice: x: 2, y: 2, z: 4, core: 2. Of those that a mesh axis runs over, the one named last changes fastest.
Arguments:
- mentor_score_matrix: bfloat16 [512, 30720], P('dp', 'vocab'), may hold values from -12 to 512
- learner_score_matrix: bfloat16 [512, 65536], P('dp', 'vocab'), may hold values from -12 to 512
- align_dev: int32 [480, 2], P('vocab'), may hold values from 0 to 15, all different within a row; in each aligned block of 30 rows (0 to 29, 30 to 59, ...) at most 5 rows name the same one
- align_slot: int32 [480, 2], P('vocab'), may hold values from 0 to 63
- align_weight: bfloat16 [480, 2, 4096], P('vocab'), may hold values from 0.00077819824 to 0.015625
Outputs:
- scaled_grad: bfloat16 [512, 65536], P('dp', 'vocab')
- divergence_penalty_result: float32 [], replicated
Inputs may be any that keep to these rules, and one draw needn't show every extreme that they name: `align_dev`: the 30 teacher blocks of one vocab shard name each owner at most 5 times in all, and in every draw some shard names some owner exactly 5 times; the 2 owners of one teacher block differ.
All inputs are finite; a program needn't handle non-finite values.
Results may differ from a plain program's by a relative error of at most 0.0039.
Values may be sent and summed in bfloat16 or wider, within the bound.
A program may use at most 64 MiB of HBM per device.

v0:
```python
import jax
import jax.numpy as jnp
from jax import lax
from jax.sharding import PartitionSpec as P

BLK = 64
SMOOTHING_HEAT = 2


def per_device(mentor_score_matrix, learner_score_matrix, align_dev, align_slot, align_weight):
    smoothing_heat_value = float(SMOOTHING_HEAT)
    owners = lax.axis_size("vocab")
    row_count = mentor_score_matrix.shape[0]
    tb_local = align_dev.shape[0]
    topk = align_dev.shape[1]
    edge_count = tb_local * topk
    most = max(2, 3 * tb_local * topk // (2 * owners))
    sb_local = learner_score_matrix.shape[1] // BLK
    slot_total = owners * most
    mentor_smoothed_scores = mentor_score_matrix.astype(jnp.float32) / smoothing_heat_value
    teacher_local = jnp.max(mentor_smoothed_scores, axis=1)
    teacher_high = lax.pmax(teacher_local, "vocab")
    teacher_exp = jnp.exp(mentor_smoothed_scores - teacher_high[:, None])
    teacher_sum = lax.psum(jnp.sum(teacher_exp, axis=1), "vocab")
    teacher_probs = (teacher_exp / teacher_sum[:, None]).astype(jnp.bfloat16)
    edge_dest = align_dev.reshape(-1)
    dest_hits = (edge_dest[:, None] == jnp.arange(owners, dtype=jnp.int32)[None, :]).astype(
        jnp.int32
    )
    earlier = jnp.sum((jnp.cumsum(dest_hits, axis=0) - dest_hits) * dest_hits, axis=1)
    position = edge_dest * most + earlier
    slot_code = (
        jnp.full((slot_total,), -1.0, jnp.float32)
        .at[position]
        .set(align_slot.reshape(-1).astype(jnp.float32))
        .astype(jnp.bfloat16)
    )
    prob_blocks = teacher_probs.reshape(row_count, tb_local, BLK)
    weight_blocks = align_weight.reshape(tb_local, topk, BLK, BLK)
    edge_terms = (
        jnp.einsum("rbc,bkcd->bkrd", prob_blocks, weight_blocks, preferred_element_type=jnp.float32)
        .astype(jnp.bfloat16)
        .reshape(edge_count, row_count * BLK)
    )
    outgoing = jnp.zeros((slot_total, row_count * BLK), jnp.bfloat16).at[position].set(edge_terms)
    arrived, arrived_code = (
        lax.all_to_all(
            outgoing.reshape(owners, most, row_count * BLK),
            "vocab",
            split_axis=0,
            concat_axis=0,
            tiled=True,
        ),
        lax.all_to_all(
            slot_code.reshape(owners, most), "vocab", split_axis=0, concat_axis=0, tiled=True
        ),
    )
    slot_terms = arrived.reshape(slot_total, row_count, BLK)
    received_code = arrived_code.reshape(-1).astype(jnp.float32)
    learner_smoothed_scores = learner_score_matrix.astype(jnp.float32) / smoothing_heat_value
    student_local = jnp.max(learner_smoothed_scores, axis=1)
    selector = (received_code[:, None] == jnp.arange(sb_local, dtype=jnp.float32)[None, :]).astype(
        jnp.bfloat16
    )
    target = jnp.einsum(
        "ps,prc->rsc", selector, slot_terms, preferred_element_type=jnp.float32
    ).reshape(row_count, sb_local * BLK)
    mass_local = jnp.sum(target, axis=1)
    student_high = lax.pmax(student_local, "vocab")
    student_exp = jnp.exp(learner_smoothed_scores - student_high[:, None])
    student_sum, target_total = lax.psum((jnp.sum(student_exp, axis=1), mass_local), "vocab")
    student_logprob = learner_smoothed_scores - (student_high + jnp.log(student_sum))[:, None]
    vocab_width = float(sb_local * BLK * owners)
    scaled_grad = (
        vocab_width * (target_total[:, None] * jnp.exp(student_logprob) - target)
    ).astype(jnp.bfloat16)
    local_loss = jnp.sum(jax.scipy.special.xlogy(target, target) - target * student_logprob)
    aggregate_divergence = lax.psum(local_loss, ("dp", "vocab"))
    symbol_number_value = float(row_count * lax.axis_size("dp"))
    divergence_penalty_result = (
        smoothing_heat_value * smoothing_heat_value * aggregate_divergence / symbol_number_value
    )
    return (scaled_grad, divergence_penalty_result)


def solution(mesh):
    in_specs = (
        P("dp", "vocab"),
        P("dp", "vocab"),
        P("vocab", None),
        P("vocab", None),
        P("vocab", None, None),
    )
    out_specs = (P("dp", "vocab"), P())
    return jax.shard_map(
        per_device, mesh=mesh, in_specs=in_specs, out_specs=out_specs, check_vma=False
    )
```

profile of v0, /device:TPU:0, one launch (start us, length us, event | category | flops | bytes accessed | tf_op | source)
XLA Modules:
  0.0 325.5 jit_solution(16581234377188281575)
XLA Ops:
  0.6 0.8 copy.23
  1.4 0.7 broadcast_multiply_fusion
  2.1 0.1 eq.28
  2.2 0.1 fusion.12
  2.3 0.1 reduce_window_sum.11
  2.4 0.2 select_reduce_fusion
  2.5 0.1 copy.22
  2.6 0.1 mul.41
  2.8 0.7 convert_element_type.46
  3.4 0.1 copy.27
  3.5 0.1 reshape.91
  3.7 0.8 scatter_custom_fusion.1
  4.4 0.7 all_to_all.12
  5.1 8.3 %all-to-all-start.1 = ((bf16[16,1,5]{2,1,0:T(2,128)(2,1)}), bf16[16,1,5]{2,1,0:T(2,128)(2,1)S(1)}, u32[]{:S(2)}, u32[]{:S(2)}) async-start(bf16[16,1,5]{2,1,0:T(2,128)(2,1)} %all_to_all.12), calls=%async_computation.1 | async-start | bytes 16384 | tf_op jit(solution)/shard_map/all_to_all | solution.py:54
  13.5 3.3 %copy.30 = bf16[256,4096]{0,1:T(8,128)(2,1)S(1)} copy(bf16[256,4096]{1,0:T(8,128)(2,1)} %param.6) | data formatting | bytes 4194304 | tf_op args[1]
  16.7 0.6 fusion.6
  17.3 1.6 copy.24
  18.9 0.3 fusion.8
  19.2 42.1 %all-reduce.1 = (f32[256]{0:T(256)S(1)}, f32[256]{0:T(256)S(1)}) all-reduce(f32[256]{0:T(256)S(1)} %fusion.8, f32[256]{0:T(256)S(1)} %fusion.6), channel_id=1, replica_groups=mesh['dp'=2,'vocab'=16] {'vocab'}, use_global_device_ids=true, to_apply=%region_3.0 | all-reduce | flops 512 | bytes 4096 | tf_op jit(solution)/shard_map/pmax | solution.py:22
  61.3 0.4 fusion.9
  61.7 36.6 %psum.28 = f32[256]{0:T(256)S(1)} all-reduce(f32[256]{0:T(256)S(1)} %fusion.9), channel_id=1, replica_groups=mesh['dp'=2,'vocab'=16] {'vocab'}, use_global_device_ids=true, to_apply=%region_5.6 | all-reduce | flops 256 | bytes 2048 | tf_op jit(solution)/shard_map/psum | solution.py:24
  98.3 1.4 divide_convert_fusion
  99.7 0.0 copy-start
  99.7 3.0 reshape.73
  102.7 2.2 copy.25
  104.9 0.0 copy-done
  104.9 1.8 fusion.21
  106.8 1.6 convert_bitcast_fusion
  108.3 4.7 %copy.26 = bf16[30,2,256,64]{3,2,1,0:T(8,128)(2,1)} copy(bf16[30,2,256,64]{2,3,1,0:T(8,128)(2,1)} %convert_bitcast_fusion) | data formatting | bytes 3932160 | tf_op jit(solution)/shard_map/convert_element_type | solution.py:42
  113.0 5.9 %reshape.83 = bf16[60,16384]{1,0:T(8,128)(2,1)} reshape(bf16[30,2,256,64]{3,2,1,0:T(8,128)(2,1)} %copy.26) | data formatting | bytes 3932160 | tf_op jit(solution)/shard_map/reshape | solution.py:43
  118.9 6.0 %scatter_custom_fusion = bf16[80,16384]{1,0:T(8,128)(2,1)} fusion(s32[60]{0:T(128)S(1)} %fusion.17, bf16[60,16384]{1,0:T(8,128)(2,1)} %reshape.83, bf16[]{:T(256)} %constant.10.clone.1), kind=kCustom, calls=%fused_computation.23 | custom fusion | bytes 2621952 | tf_op jit(solution)/shard_map/scatter | solution.py:45
  125.0 3.8 %reshape.75 = bf16[16,5,16384]{2,1,0:T(8,128)(2,1)} reshape(bf16[80,16384]{1,0:T(8,128)(2,1)} %scatter_custom_fusion) | data formatting | bytes 5242880 | tf_op jit(solution)/shard_map/reshape | solution.py:48
  128.8 0.0 all-to-all-done.1
  128.8 4.7 %all-to-all-start = ((bf16[16,5,16384]{2,1,0:T(8,128)(2,1)}), bf16[16,5,16384]{2,1,0:T(8,128)(2,1)}, u32[]{:S(2)}, u32[]{:S(2)}) async-start(bf16[16,5,16384]{2,1,0:T(8,128)(2,1)} %reshape.75), calls=%async_computation | async-start | bytes 8388608 | tf_op jit(solution)/shard_map/all_to_all | solution.py:47
  133.6 0.9 exponential_reduce_fusion
  134.5 0.1 reshape.78
  134.6 69.8 %all-to-all-done = bf16[16,5,16384]{2,1,0:T(8,128)(2,1)} async-done(((bf16[16,5,16384]{2,1,0:T(8,128)(2,1)}), bf16[16,5,16384]{2,1,0:T(8,128)(2,1)}, u32[]{:S(2)}, u32[]{:S(2)}) %all-to-all-start) | async-done | bytes 2621472 | tf_op jit(solution)/shard_map/all_to_all | solution.py:47
  204.4 9.4 %reshape.76 = bf16[80,256,64]{2,1,0:T(8,128)(2,1)} reshape(bf16[16,5,16384]{2,1,0:T(8,128)(2,1)} %all-to-all-done) | data formatting | bytes 5242880 | tf_op jit(solution)/shard_map/reshape | solution.py:58
  213.8 7.0 %copy.29 = bf16[80,256,64]{1,0,2:T(8,128)(2,1)} copy(bf16[80,256,64]{2,1,0:T(8,128)(2,1)} %reshape.76) | data formatting | bytes 5242880 | tf_op jit(solution)/shard_map/reshape | solution.py:58
  220.8 4.6 %fusion.20 = (f32[256]{0:T(256)S(1)}, f32[256,64,64]{0,2,1:T(8,128)}) fusion(bf16[80,256,64]{1,0,2:T(8,128)(2,1)} %copy.29, f32[80]{0:T(128)S(1)} %reshape.78), kind=kOutput, calls=%fused_computation.40 | convolution fusion | flops 168825600 | bytes 6817088 | tf_op jit(solution)/shard_map/ps,prc->rsc/dot_general | solution.py:65
  225.3 48.3 %all-reduce = (f32[256]{0:T(256)S(1)}, f32[256]{0:T(256)S(1)}) all-reduce(f32[256]{0:T(256)S(1)} %exponential_reduce_fusion, f32[256]{0:T(256)S(1)} %get-tuple-element.12), channel_id=1, replica_groups=mesh['dp'=2,'vocab'=16] {'vocab'}, use_global_device_ids=true, to_apply=%region_13.14 | all-reduce | flops 512 | bytes 4096 | tf_op jit(solution)/shard_map/psum | solution.py:71
  273.6 4.6 %copy.31 = f32[256,64,64]{0,2,1:T(8,128)S(1)} copy(f32[256,64,64]{0,1,2:T(8,128)} %bitcast.42) | data formatting | bytes 8388608 | tf_op jit(solution)/shard_map/ps,prc->rsc/transpose | solution.py:65
  278.3 4.4 %fusion.2 = (f32[]{:T(128)}, bf16[256,4096]{0,1:T(8,128)(2,1)}) fusion(f32[256,64,64]{0,2,1:T(8,128)S(1)} %copy.31, bf16[256,4096]{0,1:T(8,128)(2,1)S(1)} %copy.30, f32[256]{0:T(256)S(1)} %log_add_fusion, f32[256]{0:T(256)S(1)} %get-tuple-element.7), kind=kLoop, calls=%fused_computation.5 | loop fusion | flops 15728639 | bytes 8390660 | tf_op jit(solution)/shard_map/reduce_sum | solution.py:77
  282.6 4.1 %copy.32 = bf16[256,4096]{1,0:T(8,128)(2,1)} copy(bf16[256,4096]{0,1:T(8,128)(2,1)} %get-tuple-element.11) | data formatting | bytes 4194304
  286.7 37.1 %psum.31 = f32[]{:T(128)} all-reduce(f32[]{:T(128)} %get-tuple-element.10), channel_id=1, replica_groups=mesh['dp'=2,'vocab'=16] {'dp','vocab'}, use_global_device_ids=true, to_apply=%region_15.16 | all-reduce | flops 1 | bytes 8 | tf_op jit(solution)/shard_map/psum | solution.py:78
  (4 shorter events, 0.0 us)
Async XLA Ops:
  5.1 123.7 %all-to-all-start.1 = ((bf16[16,1,5]{2,1,0:T(2,128)(2,1)}), bf16[16,1,5]{2,1,0:T(2,128)(2,1)S(1)}, u32[]{:S(2)}, u32[]{:S(2)}) async-start(bf16[16,1,5]{2,1,0:T(2,128)(2,1)} %all_to_all.12), calls=%async_computation.1 | async-start | bytes 16384 | tf_op jit(solution)/shard_map/all_to_all | solution.py:54
  99.7 5.3 %copy-start = (bf16[256,1920]{0,1:T(8,128)(2,1)S(1)}, bf16[256,1920]{0,1:T(8,128)(2,1)}, u32[]{:S(2)}) copy-start(bf16[256,1920]{0,1:T(8,128)(2,1)} %divide_convert_fusion) | copy-start | bytes 2949124
  128.8 75.5 %all-to-all-start = ((bf16[16,5,16384]{2,1,0:T(8,128)(2,1)}), bf16[16,5,16384]{2,1,0:T(8,128)(2,1)}, u32[]{:S(2)}, u32[]{:S(2)}) async-start(bf16[16,5,16384]{2,1,0:T(8,128)(2,1)} %reshape.75), calls=%async_computation | async-start | bytes 8388608 | tf_op jit(solution)/shard_map/all_to_all | solution.py:47
where the time goes:
time: 328 us; the launch traced here: 326 us
  blocking collectives  164 us (50%)
  waiting for transfers between devices  69.8 us (21%)
  local copies, waits for them, and re-layouts  58.5 us (18%)
  starting transfers between devices  13 us (4%)
  other arithmetic  11.3 us (3%)
  matrix products  6.41 us (2%)
    all_to_all x1, waiting for transfers between devices, per_device(): lax.all_to_all(outgoing.reshape(owners, most, row_count * BLK), 'vocab',...  69.8 us
    psum x1, blocking collectives, per_device(): lax.psum((jnp.sum(student_exp, axis=1), mass_local), 'vocab')  48.3 us
    pmax x1, blocking collectives, per_device(): teacher_high = lax.pmax(teacher_local, 'vocab')  42.1 us
    psum x1, blocking collectives, per_device(): aggregate_divergence = lax.psum(local_loss, ('dp', 'vocab'))  37.1 us
    psum x1, blocking collectives, per_device(): teacher_sum = lax.psum(jnp.sum(teacher_exp, axis=1), 'vocab')  36.6 us
    reshape x2, local copies, waits for them, and re-layouts, per_device(): slot_terms = arrived.reshape(slot_total, row_count, BLK)  16.4 us
    unnamed x6, local copies, waits for them, and re-layouts  9.7 us
    all_to_all x1, starting transfers between devices, per_device(): lax.all_to_all(slot_code.reshape(owners, most), 'vocab', split_axis=0, co...  8.31 us
  transfers between devices with their start and end apart: 2, of which 1 were waited for; matrix products, arithmetic and copies ran while one was open for 12% of the time, Pallas kernels for 0%

commit v1 on v0

v1 whole, which is shorter than its diff:
```python
import functools

import jax
import jax.numpy as jnp
from jax import lax
from jax.experimental import pallas as pl
from jax.experimental.pallas import tpu as pltpu
from jax.sharding import PartitionSpec as P

BLK = 64
SMOOTHING_HEAT = 2
LANES = 128
STATS = 8
CODE_ROW = 5
VMEM_BYTES = 48 * 1024 * 1024
MESH = pl.DeviceIdType.MESH


def low_lanes(shape):
    return lax.broadcasted_iota(jnp.int32, shape, len(shape) - 1) < BLK


def columns_to_rows(columns, first, count):
    rows = columns[0].shape[0]
    lane = lax.broadcasted_iota(jnp.int32, (rows, LANES), 1)
    table = jnp.zeros((rows, LANES), jnp.float32)
    for at, column in enumerate(columns):
        table = jnp.where(lane == first + at, column, table)
    return jnp.transpose(table)[:count]


def teacher_kernel(owners, most, dev_ref, slot_ref, mentor_ref, weight_ref, out_ref, stats_ref, count_ref, place_ref):
    row_count, width = mentor_ref.shape
    half = row_count // 2
    topk = dev_ref.shape[1]
    tb_local = dev_ref.shape[0]

    for owner in range(owners):
        count_ref[owner] = 0
    code_lane = lax.broadcasted_iota(jnp.int32, (1, row_count), 1)

    def place(b, codes):
        for k in range(topk):
            owner = dev_ref[b, k]
            earlier = count_ref[owner]
            count_ref[owner] = earlier + 1
            position = owner * most + earlier
            place_ref[b * topk + k] = position
            codes = jnp.where(code_lane == position, slot_ref[b, k].astype(jnp.float32), codes)
        return codes

    codes = lax.fori_loop(0, tb_local, place, jnp.full((1, row_count), -1.0, jnp.float32))

    tiles = width // LANES
    high = mentor_ref[:, :LANES]
    for tile in range(1, tiles):
        high = jnp.maximum(high, mentor_ref[:, tile * LANES:(tile + 1) * LANES])
    high = jnp.max(high.astype(jnp.float32), axis=1, keepdims=True) / float(SMOOTHING_HEAT)

    low = low_lanes((BLK, LANES))
    none = jnp.zeros((BLK, LANES), jnp.bfloat16)

    def pair(j, carry):
        total, mass = carry
        x = mentor_ref[:, pl.ds(pl.multiple_of(j * LANES, LANES), LANES)].astype(jnp.float32)
        e = jnp.exp(x / float(SMOOTHING_HEAT) - high)
        total = total + e
        e = e.astype(jnp.bfloat16)
        lhs = jnp.concatenate([e[:half], e[half:]], axis=1)
        lefts, rights = [], []
        for b in range(2):
            blocks = [weight_ref[(2 * j + b) * topk + k] for k in range(topk)]
            pad_before, pad_after = [none] * (topk * b), [none] * (topk * (1 - b))
            lefts.append(jnp.concatenate(pad_before + [jnp.where(low, w, none) for w in blocks] + pad_after, axis=1))
            rights.append(jnp.concatenate(pad_before + [jnp.where(low, none, w) for w in blocks] + pad_after, axis=1))
        rhs = jnp.concatenate(lefts + rights, axis=0)
        terms = jnp.dot(lhs, rhs, preferred_element_type=jnp.float32).astype(jnp.bfloat16)
        for at in range(2 * topk):
            term = terms[:, at * LANES:(at + 1) * LANES]
            out_ref[place_ref[2 * topk * j + at]] = term
            mass = mass + term.astype(jnp.float32)
        return total, mass

    total, mass = lax.fori_loop(
        0, tiles, pair,
        (jnp.zeros((row_count, LANES), jnp.float32), jnp.zeros((half, LANES), jnp.float32)),
    )
    low = low_lanes((half, LANES))
    mass = jnp.concatenate([
        jnp.sum(jnp.where(low, mass, 0.0), axis=1, keepdims=True),
        jnp.sum(jnp.where(low, 0.0, mass), axis=1, keepdims=True),
    ], axis=0)
    total = jnp.sum(total, axis=1, keepdims=True)
    rows = columns_to_rows([high, total, mass], 0, STATS)
    row = lax.broadcasted_iota(jnp.int32, (STATS, row_count), 0)
    stats_ref[...] = jnp.where(row == CODE_ROW, codes, rows)


def exchange_kernel(owners, out_ref, stats_ref, learner_ref, recv_ref, cols_ref, codes_ref,
                    learner, message, table, send, recv, small_send, small_recv, local):
    dp, me = lax.axis_index("dp"), lax.axis_index("vocab")
    row_count = learner.shape[0]
    load = pltpu.make_async_copy(learner_ref, learner, local.at[0])
    load.start()
    own = pltpu.make_async_copy(out_ref.at[me], recv_ref.at[me], local.at[1])
    own.start()

    barrier = pltpu.get_barrier_semaphore()

    def greet(k, carry):
        pl.semaphore_signal(barrier, inc=1, device_id=(dp, lax.rem(me + k, owners)), device_id_type=MESH)
        return carry

    lax.fori_loop(1, owners, greet, 0)
    pl.semaphore_wait(barrier, owners - 1)

    def block_copy(k):
        peer = lax.rem(me + k, owners)
        return pltpu.make_async_remote_copy(
            src_ref=out_ref.at[peer], dst_ref=recv_ref.at[me], send_sem=send.at[k], recv_sem=recv.at[k],
            device_id=(dp, peer), device_id_type=MESH)

    def small_copy(k):
        peer = lax.rem(me + k, owners)
        return pltpu.make_async_remote_copy(
            src_ref=message, dst_ref=table.at[me], send_sem=small_send.at[k], recv_sem=small_recv.at[k],
            device_id=(dp, peer), device_id_type=MESH)

    def start_block(k, carry):
        block_copy(k).start()
        return carry

    lax.fori_loop(1, owners, start_block, 0)

    load.wait()
    tiles = learner.shape[1] // LANES

    def tile_of(j):
        return learner[:, pl.ds(pl.multiple_of(j * LANES, LANES), LANES)]

    high = lax.fori_loop(1, tiles, lambda j, h: jnp.maximum(h, tile_of(j)), learner[:, :LANES])
    high = jnp.max(high.astype(jnp.float32), axis=1, keepdims=True) / float(SMOOTHING_HEAT)

    def add_exp(j, total):
        return total + jnp.exp(tile_of(j).astype(jnp.float32) / float(SMOOTHING_HEAT) - high)

    total = lax.fori_loop(0, tiles, add_exp, jnp.zeros((row_count, LANES), jnp.float32))
    total = jnp.sum(total, axis=1, keepdims=True)
    message[...] = stats_ref[...] + columns_to_rows([high, total], 3, STATS)
    table[me] = message[...]

    def start_small(k, carry):
        small_copy(k).start()
        return carry

    def wait_small(k, carry):
        small_copy(k).wait()
        return carry

    lax.fori_loop(1, owners, start_small, 0)
    lax.fori_loop(1, owners, wait_small, 0)

    teacher_high = table[:, 0, :]
    teacher_scale = jnp.exp(teacher_high - jnp.max(teacher_high, axis=0, keepdims=True))
    weight = teacher_scale / jnp.sum(table[:, 1, :] * teacher_scale, axis=0, keepdims=True)
    target_total = jnp.sum(table[:, 2, :] * weight, axis=0, keepdims=True)
    student_high = table[:, 3, :]
    top = jnp.max(student_high, axis=0, keepdims=True)
    student_lse = top + jnp.log(jnp.sum(table[:, 4, :] * jnp.exp(student_high - top), axis=0, keepdims=True))
    fill = jnp.zeros((LANES - owners - STATS, row_count), jnp.float32)
    row = lax.broadcasted_iota(jnp.int32, (STATS, row_count), 0)
    tail = jnp.where(row == 0, target_total, jnp.where(row == 1, student_lse, 0.0))
    cols_ref[...] = jnp.transpose(jnp.concatenate([weight, tail, fill], axis=0))
    codes_ref[...] = table[:, CODE_ROW, :]

    def wait_block(k, carry):
        block_copy(k).wait()
        return carry

    lax.fori_loop(1, owners, wait_block, 0)
    own.wait()


def student_kernel(owners, most, codes_ref, recv_ref, cols_ref, learner_ref, grad_ref, loss_ref, target_ref):
    me = lax.axis_index("vocab")
    row_count, width = learner_ref.shape
    half = row_count // 2
    sb_local = width // BLK
    vocab_width = float(width * owners)

    def clear(c, carry):
        target_ref[c] = jnp.zeros((half, LANES), jnp.float32)
        return carry

    lax.fori_loop(0, sb_local, clear, 0)
    low = low_lanes((half, LANES))
    for source in range(owners):
        column = cols_ref[:, source:source + 1]
        scale = jnp.where(low, column[:half], column[half:])
        for at in range(most):
            code = codes_ref[source, me * most + at].astype(jnp.int32)
            block = jnp.where(code < 0, sb_local, code)
            target_ref[block] = target_ref[block] + recv_ref[source, at].astype(jnp.float32) * scale

    target_total = cols_ref[:, owners:owners + 1] * vocab_width
    lse = cols_ref[:, owners + 1:owners + 2]

    def pair(j, loss):
        first, second = target_ref[2 * j], target_ref[2 * j + 1]
        target = jnp.concatenate([
            jnp.where(low, first, pltpu.roll(second, BLK, 1)),
            jnp.where(low, pltpu.roll(first, BLK, 1), second),
        ], axis=0)
        at = pl.ds(pl.multiple_of(j * LANES, LANES), LANES)
        logprob = learner_ref[:, at].astype(jnp.float32) / float(SMOOTHING_HEAT) - lse
        grad_ref[:, at] = (target_total * jnp.exp(logprob) - vocab_width * target).astype(jnp.bfloat16)
        fed = target > 0.0
        return loss + jnp.where(fed, target * (jnp.log(jnp.where(fed, target, 1.0)) - logprob), 0.0)

    loss = lax.fori_loop(0, sb_local // 2, pair, jnp.zeros((row_count, LANES), jnp.float32))
    loss_ref[...] = jnp.sum(loss.reshape(row_count // 8, 8, LANES), axis=0)


def loss_kernel(parts, owners, scale, loss_ref, result_ref, table, send, recv):
    me = lax.axis_index("dp") * owners + lax.axis_index("vocab")
    everyone = parts * owners

    def device(k):
        peer = lax.rem(me + k, everyone)
        return (peer // owners, lax.rem(peer, owners))

    barrier = pltpu.get_barrier_semaphore()

    def greet(k, carry):
        pl.semaphore_signal(barrier, inc=1, device_id=device(k), device_id_type=MESH)
        return carry

    lax.fori_loop(1, everyone, greet, 0)
    table[me] = loss_ref[...]
    pl.semaphore_wait(barrier, everyone - 1)

    def copy(k):
        return pltpu.make_async_remote_copy(
            src_ref=loss_ref, dst_ref=table.at[me], send_sem=send.at[k], recv_sem=recv.at[k],
            device_id=device(k), device_id_type=MESH)

    def start(k, carry):
        copy(k).start()
        return carry

    def wait(k, carry):
        copy(k).wait()
        return carry

    lax.fori_loop(1, everyone, start, 0)
    lax.fori_loop(1, everyone, wait, 0)
    total = jnp.sum(table[...], axis=0)
    total = jnp.sum(jnp.sum(total, axis=0, keepdims=True), axis=1, keepdims=True)
    result_ref[...] = total * scale


def per_device(mentor_score_matrix, learner_score_matrix, align_dev, align_slot, align_weight):
    parts, owners = lax.axis_size("dp"), lax.axis_size("vocab")
    row_count, _ = mentor_score_matrix.shape
    half = row_count // 2
    tb_local, topk = align_dev.shape
    most = max(2, 3 * tb_local * topk // (2 * owners))
    width = learner_score_matrix.shape[1]
    sb_local = width // BLK
    vmem = pl.BlockSpec(memory_space=pltpu.VMEM)
    smem = pl.BlockSpec(memory_space=pltpu.SMEM)
    anywhere = pl.BlockSpec(memory_space=pl.ANY)

    weight = align_weight.reshape(tb_local * topk, BLK, BLK)
    weight = jnp.concatenate([weight, weight], axis=2)

    outgoing, stats = pl.pallas_call(
        functools.partial(teacher_kernel, owners, most),
        out_shape=(
            jax.ShapeDtypeStruct((owners * most, half, LANES), jnp.bfloat16),
            jax.ShapeDtypeStruct((STATS, row_count), jnp.float32),
        ),
        in_specs=[smem, smem, vmem, vmem],
        out_specs=(vmem, vmem),
        scratch_shapes=[pltpu.SMEM((owners,), jnp.int32), pltpu.SMEM((tb_local * topk,), jnp.int32)],
        compiler_params=pltpu.CompilerParams(vmem_limit_bytes=VMEM_BYTES),
        name="teacher_terms",
    )(align_dev, align_slot, mentor_score_matrix, weight)

    arrived, columns, codes = pl.pallas_call(
        functools.partial(exchange_kernel, owners),
        out_shape=(
            jax.ShapeDtypeStruct((owners, most, half, LANES), jnp.bfloat16),
            jax.ShapeDtypeStruct((row_count, LANES), jnp.float32),
            jax.ShapeDtypeStruct((owners, row_count), jnp.float32),
        ),
        in_specs=[anywhere, vmem, anywhere],
        out_specs=(anywhere, vmem, vmem),
        scratch_shapes=[
            pltpu.VMEM((row_count, width), jnp.bfloat16),
            pltpu.VMEM((STATS, row_count), jnp.float32),
            pltpu.VMEM((owners, STATS, row_count), jnp.float32),
            pltpu.SemaphoreType.DMA((owners,)),
            pltpu.SemaphoreType.DMA((owners,)),
            pltpu.SemaphoreType.DMA((owners,)),
            pltpu.SemaphoreType.DMA((owners,)),
            pltpu.SemaphoreType.DMA((2,)),
        ],
        compiler_params=pltpu.CompilerParams(
            collective_id=0, has_side_effects=True, vmem_limit_bytes=VMEM_BYTES),
        name="exchange",
    )(outgoing.reshape(owners, most, half, LANES), stats, learner_score_matrix)

    scaled_grad, loss = pl.pallas_call(
        functools.partial(student_kernel, owners, most),
        out_shape=(
            jax.ShapeDtypeStruct((row_count, width), jnp.bfloat16),
            jax.ShapeDtypeStruct((8, LANES), jnp.float32),
        ),
        in_specs=[smem, vmem, vmem, vmem],
        out_specs=(vmem, vmem),
        scratch_shapes=[pltpu.VMEM((sb_local + 1, half, LANES), jnp.float32)],
        compiler_params=pltpu.CompilerParams(vmem_limit_bytes=VMEM_BYTES),
        name="student_gradient",
    )(codes, arrived, columns, learner_score_matrix)

    scale = float(SMOOTHING_HEAT) * float(SMOOTHING_HEAT) / float(row_count * parts)
    total = pl.pallas_call(
        functools.partial(loss_kernel, parts, owners, scale),
        out_shape=jax.ShapeDtypeStruct((1, 1), jnp.float32),
        in_specs=[vmem],
        out_specs=vmem,
        scratch_shapes=[
            pltpu.VMEM((parts * owners, 8, LANES), jnp.float32),
            pltpu.SemaphoreType.DMA((parts * owners,)),
            pltpu.SemaphoreType.DMA((parts * owners,)),
        ],
        compiler_params=pltpu.CompilerParams(collective_id=1, has_side_effects=True),
        name="loss_sum",
    )(loss)
    return scaled_grad, total[0, 0]


def solution(mesh):
    in_specs = (
        P("dp", "vocab"),
        P("dp", "vocab"),
        P("vocab", None),
        P("vocab", None),
        P("vocab", None, None),
    )
    out_specs = (P("dp", "vocab"), P())
    return jax.shard_map(
        per_device, mesh=mesh, in_specs=in_specs, out_specs=out_specs, check_vma=False
    )
```

time: 328 us -> 106 us (0.32)
  blocking collectives: 164 us -> 0 us
  Pallas kernels: 0 us -> 97 us
  waiting for transfers between devices: 69.8 us -> 0 us
  local copies, waits for them, and re-layouts: 58.5 us -> 5.98 us
  starting transfers between devices: 13 us -> 0 us
  other arithmetic: 11.3 us -> 0.54 us
  matrix products: 6.41 us -> 0 us
    psum x3 -> x0, blocking collectives: 122 us -> none  [the longest x1 48.3 us: per_device(): lax.psum((jnp.sum(student_exp, axis=1), mass_local), 'vocab')]
    pallas_call x0 -> x4, Pallas kernels: none -> 97 us  [the longest x1 72.3 us: per_device(): pl.pallas_call(functools.partial(exchange_kernel, owners), out_shape=(jax...]
    all_to_all x2 -> x0, waiting for transfers between devices: 69.8 us -> none  [the longest x1 69.8 us: per_device(): lax.all_to_all(outgoing.reshape(owners, most, row_count * BLK), 'vocab',...]
    pmax x1 -> x0, blocking collectives: 42.1 us -> none  [per_device(): teacher_high = lax.pmax(teacher_local, 'vocab')]
    reshape x6 -> x1, local copies, waits for them, and re-layouts: 31.4 us -> 2.21 us  [per_device(): weight = align_weight.reshape(tb_local * topk, BLK, BLK)]
    all_to_all x2 -> x0, starting transfers between devices: 13 us -> none  [the longest x1 8.31 us: per_device(): lax.all_to_all(slot_code.reshape(owners, most), 'vocab', split_axis=0, co...]
    scatter x2 -> x0, local copies, waits for them, and re-layouts: 6.81 us -> none  [the longest x1 6.05 us: per_device(): jnp.zeros((slot_total, row_count * BLK), jnp.bfloat16).at[position]]
    unnamed x6 -> x10, local copies, waits for them, and re-layouts: 9.7 us -> 3.77 us
  transfers between devices with their start and end apart: 2 -> 0, of which waited for: 1 -> 0; matrix products, arithmetic and copies ran while one was open for 12% -> 0% of each run, Pallas kernels for 0% -> 0%
where the time goes in v1:
time: 106 us
  Pallas kernels  97 us (92%)
  local copies, waits for them, and re-layouts  5.98 us (6%)
  between operations  2.37 us (2%)
    pallas_call x1, Pallas kernels, per_device(): pl.pallas_call(functools.partial(exchange_kernel, owners), out_shape=(jax...  72.3 us
    pallas_call x1, Pallas kernels, per_device(): pl.pallas_call(functools.partial(loss_kernel, parts, owners, scale), out_...  10.4 us
    pallas_call x1, Pallas kernels, per_device(): pl.pallas_call(functools.partial(student_kernel, owners, most), out_shape...  9.16 us
    pallas_call x1, Pallas kernels, per_device(): pl.pallas_call(functools.partial(teacher_kernel, owners, most), out_shape...  5.08 us
    unnamed x10, local copies, waits for them, and re-layouts  3.77 us
    reshape x1, local copies, waits for them, and re-layouts, per_device(): weight = align_weight.reshape(tb_local * topk, BLK, BLK)  2.21 us

profile of v1, /device:TPU:0, one launch (start us, length us, event | category | flops | bytes accessed | tf_op | source)
XLA Modules:
  0.0 105.9 jit_solution(2846273634772170477)
XLA Ops:
  0.6 0.0 copy-start.2
  0.6 0.9 copy.7.dev_ref
  1.5 0.8 copy.8.slot_ref
  2.3 2.2 %reshape.10 = bf16[60,64,64]{2,1,0:T(8,128)(2,1)S(1)} reshape(bf16[30,2,4096]{2,1,0:T(2,128)(2,1)} %param.9) | data formatting | bytes 983040 | tf_op jit(solution)/shard_map/reshape | solution.py:274
  4.5 0.0 copy-start
  4.5 0.5 pad_maximum_fusion.weight_ref
  5.0 0.0 copy-done.2
  5.1 5.1 %teacher_terms.1 = (bf16[80,128,128]{2,1,0:T(8,128)(2,1)S(1)}, f32[8,256]{1,0:T(8,128)S(1)}) custom-call(s32[30,2]{1,0:T(8,128)S(1)} %copy.7.dev_ref, s32[30,2]{1,0:T(8,128)S(1)} %copy.8.slot_ref, bf16[256,1920]{1,0:T(8,128)(2,1)S(1)} %copy-done.2, bf16[60,64,128]{2,1,0:T(8,128)(2,1)S(1)} %pad_maximum_fusion.weight_ref), custom_call_target="tpu_custom_call" | custom-call | tf_op jit(solution)/shard_map/teacher_terms/pallas_call | solution.py:277
  10.1 0.0 copy-start.1
  10.1 1.5 %copy-done.1 = bf16[80,128,128]{2,1,0:T(8,128)(2,1)} copy-done((bf16[80,128,128]{2,1,0:T(8,128)(2,1)}, bf16[80,128,128]{2,1,0:T(8,128)(2,1)S(1)}, u32[]{:S(2)}) %copy-start.1) | copy-done | bytes 2621464
  11.7 0.0 copy-done
  11.7 72.3 %exchange.1 = (bf16[16,5,128,128]{3,2,1,0:T(8,128)(2,1)S(1)}, f32[256,128]{1,0:T(8,128)S(1)}, f32[16,256]{1,0:T(8,128)S(1)}) custom-call(bf16[16,5,128,128]{3,2,1,0:T(8,128)(2,1)} %bitcast.2, f32[8,256]{1,0:T(8,128)S(1)} %get-tuple-element.10.stats_ref, bf16[256,4096]{1,0:T(8,128)(2,1)S(1)} %copy-done), custom_call_target="tpu_custom_call" | custom-call | tf_op jit(solution)/shard_map/exchange/pallas_call | solution.py:290
  84.0 9.2 %student_gradient.1 = (bf16[256,4096]{1,0:T(8,128)(2,1)}, f32[8,128]{1,0:T(8,128)S(1)}) custom-call(f32[16,256]{1,0:T(8,128)S(1)} %get-tuple-element.11.codes_ref, bf16[16,5,128,128]{3,2,1,0:T(8,128)(2,1)S(1)} %get-tuple-element.12.recv_ref, f32[256,128]{1,0:T(8,128)S(1)} %get-tuple-element.13.cols_ref, bf16[256,4096]{1,0:T(8,128)(2,1)S(1)} %copy-done), custom_call_target="tpu_custom_call" | custom-call | tf_op jit(solution)/shard_map/student_gradient/pallas_call | solution.py:314
  93.2 0.0 copy-start.3
  93.2 0.6 copy-done.3
  93.8 10.4 %loss_sum.1 = f32[1,1]{1,0:T(1,128)} custom-call(f32[8,128]{1,0:T(8,128)} %copy-done.3), custom_call_target="tpu_custom_call" | custom-call | tf_op jit(solution)/shard_map/loss_sum/pallas_call | solution.py:328
Async XLA Ops:
  0.6 4.4 %copy-start.2 = (bf16[256,1920]{1,0:T(8,128)(2,1)S(1)}, bf16[256,1920]{1,0:T(8,128)(2,1)}, u32[]{:S(2)}) copy-start(bf16[256,1920]{1,0:T(8,128)(2,1)} %mentor_ref.1) | copy-start | bytes 2949124
  4.5 7.2 %copy-start = (bf16[256,4096]{1,0:T(8,128)(2,1)S(1)}, bf16[256,4096]{1,0:T(8,128)(2,1)}, u32[]{:S(2)}) copy-start(bf16[256,4096]{1,0:T(8,128)(2,1)} %learner_ref.3) | copy-start | bytes 6291460
  10.1 1.5 %copy-start.1 = (bf16[80,128,128]{2,1,0:T(8,128)(2,1)}, bf16[80,128,128]{2,1,0:T(8,128)(2,1)S(1)}, u32[]{:S(2)}) copy-start(bf16[80,128,128]{2,1,0:T(8,128)(2,1)S(1)} %get-tuple-element.9) | copy-start | bytes 7864324
  93.2 0.6 copy-start.3

commit v2 on v1

--- a/solution.py
+++ b/solution.py
@@ -12,7 +12,8 @@
 LANES = 128
 STATS = 8
 CODE_ROW = 5
-VMEM_BYTES = 48 * 1024 * 1024
+OUTER = 4
+VMEM_BYTES = 24 * 1024 * 1024
 MESH = pl.DeviceIdType.MESH
 
 
@@ -32,8 +33,8 @@
 def teacher_kernel(owners, most, dev_ref, slot_ref, mentor_ref, weight_ref, out_ref, stats_ref, count_ref, place_ref):
     row_count, width = mentor_ref.shape
     half = row_count // 2
-    topk = dev_ref.shape[1]
-    tb_local = dev_ref.shape[0]
+    topk = dev_ref.shape[0]
+    tb_local = dev_ref.shape[1]
 
     for owner in range(owners):
         count_ref[owner] = 0
@@ -41,12 +42,12 @@
 
     def place(b, codes):
         for k in range(topk):
-            owner = dev_ref[b, k]
+            owner = dev_ref[k, b]
             earlier = count_ref[owner]
             count_ref[owner] = earlier + 1
             position = owner * most + earlier
             place_ref[b * topk + k] = position
-            codes = jnp.where(code_lane == position, slot_ref[b, k].astype(jnp.float32), codes)
+            codes = jnp.where(code_lane == position, slot_ref[k, b].astype(jnp.float32), codes)
         return codes
 
     codes = lax.fori_loop(0, tb_local, place, jnp.full((1, row_count), -1.0, jnp.float32))
@@ -96,6 +97,19 @@
     stats_ref[...] = jnp.where(row == CODE_ROW, codes, rows)
 
 
+def outer_partner(outer, far):
+    return (outer, outer + 1 - 2 * lax.rem(outer, 2), lax.rem(outer + 2, OUTER), OUTER - 1 - outer)[far]
+
+
+def partner_copy(owners, dp, me, out_ref, recv_ref, send, recv, far, near):
+    inner = owners // OUTER
+    peer = outer_partner(me // inner, far) * inner + lax.rem(lax.rem(me, inner) + near, inner)
+    slot = far * inner + near
+    return pltpu.make_async_remote_copy(
+        src_ref=out_ref.at[peer], dst_ref=recv_ref.at[me], send_sem=send.at[slot], recv_sem=recv.at[slot],
+        device_id=(dp, peer), device_id_type=MESH)
+
+
 def exchange_kernel(owners, out_ref, stats_ref, learner_ref, recv_ref, cols_ref, codes_ref,
                     learner, message, table, send, recv, small_send, small_recv, local):
     dp, me = lax.axis_index("dp"), lax.axis_index("vocab")
@@ -114,11 +128,7 @@
     lax.fori_loop(1, owners, greet, 0)
     pl.semaphore_wait(barrier, owners - 1)
 
-    def block_copy(k):
-        peer = lax.rem(me + k, owners)
-        return pltpu.make_async_remote_copy(
-            src_ref=out_ref.at[peer], dst_ref=recv_ref.at[me], send_sem=send.at[k], recv_sem=recv.at[k],
-            device_id=(dp, peer), device_id_type=MESH)
+    block_copy = functools.partial(partner_copy, owners, dp, me, out_ref, recv_ref, send, recv)
 
     def small_copy(k):
         peer = lax.rem(me + k, owners)
@@ -126,11 +136,16 @@
             src_ref=message, dst_ref=table.at[me], send_sem=small_send.at[k], recv_sem=small_recv.at[k],
             device_id=(dp, peer), device_id_type=MESH)
 
-    def start_block(k, carry):
-        block_copy(k).start()
-        return carry
-
-    lax.fori_loop(1, owners, start_block, 0)
+    def start_blocks(near, carry):
+        block_copy(2, near).start()
+        block_copy(1, near).start()
+        block_copy(3, near).start()
+        block_copy(0, near).start()
+        return carry
+
+    for far in (2, 1, 3):
+        block_copy(far, 0).start()
+    lax.fori_loop(1, owners // OUTER, start_blocks, 0)
 
     load.wait()
     tiles = learner.shape[1] // LANES
@@ -173,11 +188,14 @@
     cols_ref[...] = jnp.transpose(jnp.concatenate([weight, tail, fill], axis=0))
     codes_ref[...] = table[:, CODE_ROW, :]
 
-    def wait_block(k, carry):
-        block_copy(k).wait()
-        return carry
-
-    lax.fori_loop(1, owners, wait_block, 0)
+    def wait_blocks(near, carry):
+        for far in range(OUTER):
+            block_copy(far, near).wait()
+        return carry
+
+    for far in (2, 1, 3):
+        block_copy(far, 0).wait()
+    lax.fori_loop(1, owners // OUTER, wait_blocks, 0)
     own.wait()
 
 
@@ -285,7 +303,7 @@
         scratch_shapes=[pltpu.SMEM((owners,), jnp.int32), pltpu.SMEM((tb_local * topk,), jnp.int32)],
         compiler_params=pltpu.CompilerParams(vmem_limit_bytes=VMEM_BYTES),
         name="teacher_terms",
-    )(align_dev, align_slot, mentor_score_matrix, weight)
+    )(align_dev.T, align_slot.T, mentor_score_matrix, weight)
 
     arrived, columns, codes = pl.pallas_call(
         functools.partial(exchange_kernel, owners),
@@ -294,7 +312,7 @@
             jax.ShapeDtypeStruct((row_count, LANES), jnp.float32),
             jax.ShapeDtypeStruct((owners, row_count), jnp.float32),
         ),
-        in_specs=[anywhere, vmem, anywhere],
+        in_specs=[vmem, vmem, anywhere],
         out_specs=(anywhere, vmem, vmem),
         scratch_shapes=[
             pltpu.VMEM((row_count, width), jnp.bfloat16),

time: 106 us -> 99.6 us (0.940)
  Pallas kernels: 97 us -> 93.4 us
  local copies, waits for them, and re-layouts: 5.98 us -> 2.91 us
    pallas_call x1, Pallas kernels: 72.3 us -> 68.9 us  [per_device(): pl.pallas_call(functools.partial(exchange_kernel, owners), out_shape=(jax...]
    unnamed x10, local copies, waits for them, and re-layouts: 3.77 us -> 0.6 us
where the time goes in v2:
time: 99.6 us; the launch traced here: 99.4 us
  Pallas kernels  93.4 us (94%)
  local copies, waits for them, and re-layouts  2.91 us (3%)
  between operations  2.52 us (3%)
    pallas_call x1, Pallas kernels, per_device(): pl.pallas_call(functools.partial(exchange_kernel, owners), out_shape=(jax...  68.9 us
    pallas_call x1, Pallas kernels, per_device(): pl.pallas_call(functools.partial(loss_kernel, parts, owners, scale), out_...  10.7 us
    pallas_call x1, Pallas kernels, per_device(): pl.pallas_call(functools.partial(student_kernel, owners, most), out_shape...  9.16 us
    pallas_call x1, Pallas kernels, per_device(): pl.pallas_call(functools.partial(teacher_kernel, owners, most), out_shape...  4.59 us
    reshape x1, local copies, waits for them, and re-layouts, per_device(): weight = align_weight.reshape(tb_local * topk, BLK, BLK)  2.3 us

profile of v2, /device:TPU:0, one launch (start us, length us, event | category | flops | bytes accessed | tf_op | source)
XLA Modules:
  0.0 99.4 jit_solution(6215803177137867845)
XLA Ops:
  0.6 0.0 copy-start.4
  0.6 0.0 copy-start.3
  0.6 0.0 copy-start.1
  0.7 2.3 %reshape.10 = bf16[60,64,64]{2,1,0:T(8,128)(2,1)S(1)} reshape(bf16[30,2,4096]{2,1,0:T(2,128)(2,1)} %param.9) | data formatting | bytes 983040 | tf_op jit(solution)/shard_map/reshape | solution.py:292
  3.0 0.0 copy-start
  3.0 0.5 pad_maximum_fusion.weight_ref
  3.5 0.0 copy-done.4
  3.5 0.0 copy-done.3
  3.6 0.0 copy-done.1
  3.6 4.6 %teacher_terms.1 = (bf16[80,128,128]{2,1,0:T(8,128)(2,1)S(1)}, f32[8,256]{1,0:T(8,128)S(1)}) custom-call(s32[2,30]{1,0:T(2,128)S(1)} %bitcast.5, s32[2,30]{1,0:T(2,128)S(1)} %bitcast.6, bf16[256,1920]{1,0:T(8,128)(2,1)S(1)} %copy-done.1, bf16[60,64,128]{2,1,0:T(8,128)(2,1)S(1)} %pad_maximum_fusion.weight_ref), custom_call_target="tpu_custom_call" | custom-call | tf_op jit(solution)/shard_map/teacher_terms/pallas_call | solution.py:295
  8.1 0.0 copy-done
  8.2 68.9 %exchange.1 = (bf16[16,5,128,128]{3,2,1,0:T(8,128)(2,1)S(1)}, f32[256,128]{1,0:T(8,128)S(1)}, f32[16,256]{1,0:T(8,128)S(1)}) custom-call(bf16[16,5,128,128]{3,2,1,0:T(8,128)(2,1)S(1)} %bitcast.4, f32[8,256]{1,0:T(8,128)S(1)} %get-tuple-element.10.stats_ref, bf16[256,4096]{1,0:T(8,128)(2,1)S(1)} %copy-done), custom_call_target="tpu_custom_call" | custom-call | tf_op jit(solution)/shard_map/exchange/pallas_call | solution.py:308
  77.1 9.2 %student_gradient.1 = (bf16[256,4096]{1,0:T(8,128)(2,1)}, f32[8,128]{1,0:T(8,128)S(1)}) custom-call(f32[16,256]{1,0:T(8,128)S(1)} %get-tuple-element.11.codes_ref, bf16[16,5,128,128]{3,2,1,0:T(8,128)(2,1)S(1)} %get-tuple-element.12.recv_ref, f32[256,128]{1,0:T(8,128)S(1)} %get-tuple-element.13.cols_ref, bf16[256,4096]{1,0:T(8,128)(2,1)S(1)} %copy-done), custom_call_target="tpu_custom_call" | custom-call | tf_op jit(solution)/shard_map/student_gradient/pallas_call | solution.py:332
  86.3 0.0 copy-start.2
  86.3 0.6 copy-done.2
  86.9 10.7 %loss_sum.1 = f32[1,1]{1,0:T(1,128)} custom-call(f32[8,128]{1,0:T(8,128)} %copy-done.2), custom_call_target="tpu_custom_call" | custom-call | tf_op jit(solution)/shard_map/loss_sum/pallas_call | solution.py:346
Async XLA Ops:
  0.6 2.9 %copy-start.4 = (s32[30,2]{0,1:T(2,128)S(1)}, s32[30,2]{0,1:T(2,128)}, u32[]{:S(2)}) copy-start(s32[30,2]{0,1:T(2,128)} %param.8) | copy-start | bytes 724
  0.6 2.9 %copy-start.3 = (s32[30,2]{0,1:T(2,128)S(1)}, s32[30,2]{0,1:T(2,128)}, u32[]{:S(2)}) copy-start(s32[30,2]{0,1:T(2,128)} %param.7) | copy-start | bytes 724
  0.6 2.9 %copy-start.1 = (bf16[256,1920]{1,0:T(8,128)(2,1)S(1)}, bf16[256,1920]{1,0:T(8,128)(2,1)}, u32[]{:S(2)}) copy-start(bf16[256,1920]{1,0:T(8,128)(2,1)} %mentor_ref.1) | copy-start | bytes 2949124
  3.0 5.2 %copy-start = (bf16[256,4096]{1,0:T(8,128)(2,1)S(1)}, bf16[256,4096]{1,0:T(8,128)(2,1)}, u32[]{:S(2)}) copy-start(bf16[256,4096]{1,0:T(8,128)(2,1)} %learner_ref.3) | copy-start | bytes 6291460
  86.3 0.6 copy-start.2

commit v3 on v2

v3 whole, which is shorter than its diff:
```python
import functools

import jax
import jax.numpy as jnp
from jax import lax
from jax.experimental import pallas as pl
from jax.experimental.pallas import tpu as pltpu
from jax.sharding import PartitionSpec as P

BLK = 64
SMOOTHING_HEAT = 2
LANES = 128
STATS = 8
OUTER = 4
FAR = (0, 2, 1, 3)
VMEM_BYTES = 24 * 1024 * 1024
MESH = pl.DeviceIdType.MESH


def low_lanes(shape):
    return lax.broadcasted_iota(jnp.int32, shape, len(shape) - 1) < BLK


def columns_to_rows(columns, first, count):
    rows = columns[0].shape[0]
    lane = lax.broadcasted_iota(jnp.int32, (rows, LANES), 1)
    table = jnp.zeros((rows, LANES), jnp.float32)
    for at, column in enumerate(columns):
        table = jnp.where(lane == first + at, column, table)
    return jnp.transpose(table)[:count]


def teacher_kernel(owners, most, dev_ref, slot_ref, mentor_ref, weight_ref, out_ref, stats_ref, codes_ref, count_ref, place_ref):
    row_count, width = mentor_ref.shape
    half = row_count // 2
    topk = dev_ref.shape[0]
    tb_local = dev_ref.shape[1]

    for owner in range(owners):
        count_ref[owner] = 0
    code_lane = lax.broadcasted_iota(jnp.int32, (8, LANES), 1)

    def place(b, codes):
        for k in range(topk):
            owner = dev_ref[k, b]
            earlier = count_ref[owner]
            count_ref[owner] = earlier + 1
            position = owner * most + earlier
            place_ref[b * topk + k] = position
            codes = jnp.where(code_lane == position, slot_ref[k, b], codes)
        return codes

    codes_ref[...] = lax.fori_loop(0, tb_local, place, jnp.full((8, LANES), -1, jnp.int32))

    tiles = width // LANES
    high = mentor_ref[:, :LANES]
    for tile in range(1, tiles):
        high = jnp.maximum(high, mentor_ref[:, tile * LANES:(tile + 1) * LANES])
    high = jnp.max(high.astype(jnp.float32), axis=1, keepdims=True) / float(SMOOTHING_HEAT)

    low = low_lanes((BLK, LANES))
    none = jnp.zeros((BLK, LANES), jnp.bfloat16)

    def pair(j, carry):
        total, mass = carry
        x = mentor_ref[:, pl.ds(pl.multiple_of(j * LANES, LANES), LANES)].astype(jnp.float32)
        e = jnp.exp(x / float(SMOOTHING_HEAT) - high)
        total = total + e
        e = e.astype(jnp.bfloat16)
        lhs = jnp.concatenate([e[:half], e[half:]], axis=1)
        lefts, rights = [], []
        for b in range(2):
            blocks = [weight_ref[(2 * j + b) * topk + k] for k in range(topk)]
            pad_before, pad_after = [none] * (topk * b), [none] * (topk * (1 - b))
            lefts.append(jnp.concatenate(pad_before + [jnp.where(low, w, none) for w in blocks] + pad_after, axis=1))
            rights.append(jnp.concatenate(pad_before + [jnp.where(low, none, w) for w in blocks] + pad_after, axis=1))
        rhs = jnp.concatenate(lefts + rights, axis=0)
        terms = jnp.dot(lhs, rhs, preferred_element_type=jnp.float32).astype(jnp.bfloat16)
        for at in range(2 * topk):
            term = terms[:, at * LANES:(at + 1) * LANES]
            out_ref[place_ref[2 * topk * j + at]] = term
            mass = mass + term.astype(jnp.float32)
        return total, mass

    total, mass = lax.fori_loop(
        0, tiles, pair,
        (jnp.zeros((row_count, LANES), jnp.float32), jnp.zeros((half, LANES), jnp.float32)),
    )
    low = low_lanes((half, LANES))
    mass = jnp.concatenate([
        jnp.sum(jnp.where(low, mass, 0.0), axis=1, keepdims=True),
        jnp.sum(jnp.where(low, 0.0, mass), axis=1, keepdims=True),
    ], axis=0)
    total = jnp.sum(total, axis=1, keepdims=True)
    stats_ref[...] = columns_to_rows([high, total, mass], 0, STATS)


def outer_partner(outer, far):
    return (outer, outer + 1 - 2 * lax.rem(outer, 2), lax.rem(outer + 2, OUTER), OUTER - 1 - outer)[far]


def student_kernel(parts, owners, most, loss_scale,
                   out_ref, stats_ref, codes_ref, learner_ref, grad_ref, loss_ref,
                   received, sums, scale, message, teacher_table, student_table, code_table, code_smem,
                   history, history_smem, part_loss, part_table, loss_message, loss_table,
                   send, recv, local):
    dp, me = lax.axis_index("dp"), lax.axis_index("vocab")
    row_count, width = learner_ref.shape
    half = row_count // 2
    tiles = width // LANES
    slots = owners * most
    inner = owners // OUTER
    vocab_width = float(width * owners)
    low = low_lanes((half, LANES))

    def partner(near, order):
        return outer_partner(me // inner, FAR[order]) * inner + lax.rem(lax.rem(me, inner) + near, inner)

    def copy_to(kind, near, order, src, dst):
        peer = partner(near, order)
        slot = near * OUTER + order
        return pltpu.make_async_remote_copy(
            src_ref=out_ref.at[peer] if src is None else src, dst_ref=dst.at[slot],
            send_sem=send.at[kind, slot], recv_sem=recv.at[kind, slot],
            device_id=(dp, peer), device_id_type=MESH)

    def blocks(near, order):
        return copy_to(0, near, order, None, received)

    def teacher_stats(near, order):
        return copy_to(1, near, order, stats_ref, teacher_table)

    def slot_codes(near, order):
        return copy_to(2, near, order, codes_ref, code_table)

    def student_stats(near, order):
        return copy_to(3, near, order, message, student_table)

    def losses(near, order):
        return copy_to(4, near, order, loss_message, loss_table)

    def each(action):
        for order in range(1, OUTER):
            action(0, order)
        rest(action)

    def rest(action):
        def body(near, carry):
            for order in range(OUTER):
                action(near, order)
            return carry

        lax.fori_loop(1, inner, body, 0)

    def part_copy(k):
        return pltpu.make_async_remote_copy(
            src_ref=part_loss, dst_ref=part_table.at[dp], send_sem=send.at[5, k], recv_sem=recv.at[5, k],
            device_id=(lax.rem(dp + k, parts), me), device_id_type=MESH)

    barrier = pltpu.get_barrier_semaphore()

    def greet(near, order):
        pl.semaphore_signal(barrier, inc=1, device_id=(dp, partner(near, order)), device_id_type=MESH)

    each(greet)
    for k in range(1, parts):
        pl.semaphore_signal(barrier, inc=1, device_id=(lax.rem(dp + k, parts), me), device_id_type=MESH)
    pl.semaphore_wait(barrier, owners + parts - 2)

    for order in range(1, OUTER):
        blocks(0, order).start()

    def start_small(near, order):
        slot_codes(near, order).start()
        teacher_stats(near, order).start()

    each(start_small)
    rest(lambda near, order: blocks(near, order).start())

    teacher_table[0] = stats_ref[...]
    code_table[0] = codes_ref[...]

    def tile_of(j):
        return learner_ref[:, pl.ds(pl.multiple_of(j * LANES, LANES), LANES)]

    high = lax.fori_loop(1, tiles, lambda j, h: jnp.maximum(h, tile_of(j)), learner_ref[:, :LANES])
    high = jnp.max(high.astype(jnp.float32), axis=1, keepdims=True) / float(SMOOTHING_HEAT)

    def add_exp(j, total):
        return total + jnp.exp(tile_of(j).astype(jnp.float32) / float(SMOOTHING_HEAT) - high)

    total = lax.fori_loop(0, tiles, add_exp, jnp.zeros((row_count, LANES), jnp.float32))
    total = jnp.sum(total, axis=1, keepdims=True)
    message[...] = columns_to_rows([high, total], 0, STATS)
    student_table[0] = message[...]
    each(lambda near, order: student_stats(near, order).start())

    each(lambda near, order: slot_codes(near, order).wait())
    fetch = pltpu.make_async_copy(code_table, code_smem, local.at[0])
    fetch.start()
    fetch.wait()
    lane = lax.broadcasted_iota(jnp.int32, (1, LANES), 1)

    def note(q, last):
        history[pl.ds(q, 1), :] = last
        code = code_smem[q // most, 0, me * most + lax.rem(q, most)]
        return jnp.where(lane == code, q, last)

    last = lax.fori_loop(0, slots, note, jnp.full((1, LANES), slots, jnp.int32))
    history[pl.ds(slots, 1), :] = last
    fetch = pltpu.make_async_copy(history, history_smem, local.at[1])
    fetch.start()
    sums[slots] = jnp.zeros((half, LANES), jnp.float32)

    each(lambda near, order: teacher_stats(near, order).wait())
    teacher_high = teacher_table[:, 0, :]
    teacher_scale = jnp.exp(teacher_high - jnp.max(teacher_high, axis=0, keepdims=True))
    weight = teacher_scale / jnp.sum(teacher_table[:, 1, :] * teacher_scale, axis=0, keepdims=True)
    target_total = jnp.sum(teacher_table[:, 2, :] * weight, axis=0, keepdims=True)
    fill = jnp.zeros((LANES - owners - 1, row_count), jnp.float32)
    columns = jnp.transpose(jnp.concatenate([weight, target_total, fill], axis=0))
    for source in range(owners):
        column = columns[:, source:source + 1]
        scale[source] = jnp.where(low, column[:half], column[half:])
    target_total = columns[:, owners:owners + 1] * vocab_width
    fetch.wait()

    def add_blocks(slot, source_ref, index):
        for at in range(most):
            q = slot * most + at
            code = code_smem[slot, 0, me * most + at]
            earlier = sums[history_smem[q, jnp.maximum(code, 0)]]
            sums[q] = earlier + source_ref[index, at].astype(jnp.float32) * scale[slot]

    add_blocks(0, out_ref, me)

    def take(near, order):
        blocks(near, order).wait()
        slot = near * OUTER + order
        add_blocks(slot, received, slot)

    each(take)

    each(lambda near, order: student_stats(near, order).wait())
    student_high = student_table[:, 0, :]
    top = jnp.max(student_high, axis=0, keepdims=True)
    lse = top + jnp.log(jnp.sum(student_table[:, 1, :] * jnp.exp(student_high - top), axis=0, keepdims=True))
    lse = jnp.transpose(jnp.concatenate([lse, jnp.zeros((LANES - 1, row_count), jnp.float32)], axis=0))[:, :1]

    def pair(j, loss):
        first = sums[history_smem[slots, 2 * j]]
        second = sums[history_smem[slots, 2 * j + 1]]
        target = jnp.concatenate([
            jnp.where(low, first, pltpu.roll(second, BLK, 1)),
            jnp.where(low, pltpu.roll(first, BLK, 1), second),
        ], axis=0)
        at = pl.ds(pl.multiple_of(j * LANES, LANES), LANES)
        logprob = learner_ref[:, at].astype(jnp.float32) / float(SMOOTHING_HEAT) - lse
        grad_ref[:, at] = (target_total * jnp.exp(logprob) - vocab_width * target).astype(jnp.bfloat16)
        return loss + jnp.where(target > 0.0, target * (jnp.log(target) - logprob), 0.0)

    loss = lax.fori_loop(0, tiles, pair, jnp.zeros((row_count, LANES), jnp.float32))
    loss = jnp.sum(loss.reshape(row_count // 8, 8, LANES), axis=0)
    part_loss[...] = loss
    for k in range(1, parts):
        part_copy(k).start()
    part_table[dp] = loss
    for k in range(1, parts):
        part_copy(k).wait()
    loss = jnp.sum(part_table[...], axis=0)
    loss_message[...] = loss
    each(lambda near, order: losses(near, order).start())
    loss_table[0] = loss
    each(lambda near, order: losses(near, order).wait())
    totals = jnp.sum(jnp.sum(loss_table[...], axis=1), axis=1, keepdims=True)
    loss_ref[...] = jnp.sum(totals, axis=0, keepdims=True) * loss_scale


def per_device(mentor_score_matrix, learner_score_matrix, align_dev, align_slot, align_weight):
    parts, owners = lax.axis_size("dp"), lax.axis_size("vocab")
    row_count, _ = mentor_score_matrix.shape
    half = row_count // 2
    tb_local, topk = align_dev.shape
    most = max(2, 3 * tb_local * topk // (2 * owners))
    width = learner_score_matrix.shape[1]
    vmem = pl.BlockSpec(memory_space=pltpu.VMEM)
    smem = pl.BlockSpec(memory_space=pltpu.SMEM)

    weight = align_weight.reshape(tb_local * topk, BLK, BLK)
    weight = jnp.concatenate([weight, weight], axis=2)

    outgoing, stats, codes = pl.pallas_call(
        functools.partial(teacher_kernel, owners, most),
        out_shape=(
            jax.ShapeDtypeStruct((owners * most, half, LANES), jnp.bfloat16),
            jax.ShapeDtypeStruct((STATS, row_count), jnp.float32),
            jax.ShapeDtypeStruct((8, LANES), jnp.int32),
        ),
        in_specs=[smem, smem, vmem, vmem],
        out_specs=(vmem, vmem, vmem),
        scratch_shapes=[pltpu.SMEM((owners,), jnp.int32), pltpu.SMEM((tb_local * topk,), jnp.int32)],
        compiler_params=pltpu.CompilerParams(vmem_limit_bytes=VMEM_BYTES),
        name="teacher_terms",
    )(align_dev.T, align_slot.T, mentor_score_matrix, weight)

    loss_scale = float(SMOOTHING_HEAT) * float(SMOOTHING_HEAT) / float(row_count * parts)
    slots = owners * most
    history_rows = (slots // 8 + 1) * 8
    small = pltpu.VMEM((8, LANES), jnp.float32)
    scaled_grad, loss = pl.pallas_call(
        functools.partial(student_kernel, parts, owners, most, loss_scale),
        out_shape=(
            jax.ShapeDtypeStruct((row_count, width), jnp.bfloat16),
            jax.ShapeDtypeStruct((1, 1), jnp.float32),
        ),
        in_specs=[vmem, vmem, vmem, vmem],
        out_specs=(vmem, vmem),
        scratch_shapes=[
            pltpu.VMEM((owners, most, half, LANES), jnp.bfloat16),
            pltpu.VMEM((slots + 1, half, LANES), jnp.float32),
            pltpu.VMEM((owners, half, LANES), jnp.float32),
            pltpu.VMEM((STATS, row_count), jnp.float32),
            pltpu.VMEM((owners, STATS, row_count), jnp.float32),
            pltpu.VMEM((owners, STATS, row_count), jnp.float32),
            pltpu.VMEM((owners, 8, LANES), jnp.int32),
            pltpu.SMEM((owners, 8, LANES), jnp.int32),
            pltpu.VMEM((history_rows, LANES), jnp.int32),
            pltpu.SMEM((history_rows, LANES), jnp.int32),
            small,
            pltpu.VMEM((parts, 8, LANES), jnp.float32),
            small,
            pltpu.VMEM((owners, 8, LANES), jnp.float32),
            pltpu.SemaphoreType.DMA((6, owners)),
            pltpu.SemaphoreType.DMA((6, owners)),
            pltpu.SemaphoreType.DMA((2,)),
        ],
        compiler_params=pltpu.CompilerParams(
            collective_id=0, has_side_effects=True, vmem_limit_bytes=VMEM_BYTES),
        name="exchange_and_gradient",
    )(outgoing.reshape(owners, most, half, LANES), stats, codes, learner_score_matrix)
    return scaled_grad, loss[0, 0]


def solution(mesh):
    in_specs = (
        P("dp", "vocab"),
        P("dp", "vocab"),
        P("vocab", None),
        P("vocab", None),
        P("vocab", None, None),
    )
    out_specs = (P("dp", "vocab"), P())
    return jax.shard_map(
        per_device, mesh=mesh, in_specs=in_specs, out_specs=out_specs, check_vma=False
    )
```

time: 99.6 us -> 99 us (level)
  Pallas kernels: 93.4 us -> 92.2 us
    pallas_call x3 -> x1, Pallas kernels: 88.8 us -> 87.6 us  [per_device(): pl.pallas_call(functools.partial(student_kernel, parts, owners, most, los...]
where the time goes in v3:
time: 99 us; the launch traced here: 98.8 us
  Pallas kernels  92.2 us (93%)
  local copies, waits for them, and re-layouts  3.64 us (4%)
  between operations  2.4 us (2%)
    pallas_call x1, Pallas kernels, per_device(): pl.pallas_call(functools.partial(student_kernel, parts, owners, most, los...  87.6 us
    pallas_call x1, Pallas kernels, per_device(): pl.pallas_call(functools.partial(teacher_kernel, owners, most), out_shape...  4.58 us
    reshape x1, local copies, waits for them, and re-layouts, per_device(): weight = align_weight.reshape(tb_local * topk, BLK, BLK)  2.3 us

profile of v3, /device:TPU:0, one launch (start us, length us, event | category | flops | bytes accessed | tf_op | source)
XLA Modules:
  0.0 98.8 jit_solution(9557562085474431921)
XLA Ops:
  0.6 0.0 copy-start.3
  0.6 0.0 copy-start.2
  0.6 0.0 copy-start.1
  0.7 2.3 %reshape.10 = bf16[60,64,64]{2,1,0:T(8,128)(2,1)S(1)} reshape(bf16[30,2,4096]{2,1,0:T(2,128)(2,1)} %param.9) | data formatting | bytes 983040 | tf_op jit(solution)/shard_map/reshape | solution.py:289
  3.0 0.0 copy-start
  3.0 0.5 pad_maximum_fusion.weight_ref
  3.5 0.0 copy-done.3
  3.5 0.0 copy-done.2
  3.6 0.0 copy-done.1
  3.6 4.6 %teacher_terms.1 = (bf16[80,128,128]{2,1,0:T(8,128)(2,1)S(1)}, f32[8,256]{1,0:T(8,128)S(1)}, s32[8,128]{1,0:T(8,128)S(1)}) custom-call(s32[2,30]{1,0:T(2,128)S(1)} %bitcast.5, s32[2,30]{1,0:T(2,128)S(1)} %bitcast.6, bf16[256,1920]{1,0:T(8,128)(2,1)S(1)} %copy-done.1, bf16[60,64,128]{2,1,0:T(8,128)(2,1)S(1)} %pad_maximum_fusion.weight_ref), custom_call_target="tpu_custom_call" | custom-call | tf_op jit(solution)/shard_map/teacher_terms/pallas_call | solution.py:292
  8.1 0.0 copy-done
  8.1 87.6 %exchange_and_gradient.1 = (bf16[256,4096]{1,0:T(8,128)(2,1)S(1)}, f32[1,1]{1,0:T(1,128)}) custom-call(bf16[16,5,128,128]{3,2,1,0:T(8,128)(2,1)S(1)} %bitcast.4, f32[8,256]{1,0:T(8,128)S(1)} %get-tuple-element.8.stats_ref, s32[8,128]{1,0:T(8,128)S(1)} %get-tuple-element.9.codes_ref, bf16[256,4096]{1,0:T(8,128)(2,1)S(1)} %copy-done), custom_call_target="tpu_custom_call" | custom-call | tf_op jit(solution)/shard_map/exchange_and_gradient/pallas_call | solution.py:310
  95.8 1.3 %copy.9 = bf16[256,4096]{1,0:T(8,128)(2,1)} copy(bf16[256,4096]{1,0:T(8,128)(2,1)S(1)} %get-tuple-element.14) | data formatting | bytes 4194304
Async XLA Ops:
  0.6 2.9 %copy-start.3 = (s32[30,2]{0,1:T(2,128)S(1)}, s32[30,2]{0,1:T(2,128)}, u32[]{:S(2)}) copy-start(s32[30,2]{0,1:T(2,128)} %param.8) | copy-start | bytes 724
  0.6 2.9 %copy-start.2 = (s32[30,2]{0,1:T(2,128)S(1)}, s32[30,2]{0,1:T(2,128)}, u32[]{:S(2)}) copy-start(s32[30,2]{0,1:T(2,128)} %param.7) | copy-start | bytes 724
  0.6 2.9 %copy-start.1 = (bf16[256,1920]{1,0:T(8,128)(2,1)S(1)}, bf16[256,1920]{1,0:T(8,128)(2,1)}, u32[]{:S(2)}) copy-start(bf16[256,1920]{1,0:T(8,128)(2,1)} %mentor_ref.1) | copy-start | bytes 2949124
  3.0 5.2 %copy-start = (bf16[256,4096]{1,0:T(8,128)(2,1)S(1)}, bf16[256,4096]{1,0:T(8,128)(2,1)}, u32[]{:S(2)}) copy-start(bf16[256,4096]{1,0:T(8,128)(2,1)} %learner_ref.1) | copy-start | bytes 6291460

commit v4 on v3

--- a/solution.py
+++ b/solution.py
@@ -10,7 +10,9 @@
 BLK = 64
 SMOOTHING_HEAT = 2
 LANES = 128
-STATS = 8
+CHUNKS = 2
+TEACHER_STATS = 3
+STUDENT_STATS = 2
 OUTER = 4
 FAR = (0, 2, 1, 3)
 VMEM_BYTES = 24 * 1024 * 1024
@@ -21,24 +23,27 @@
     return lax.broadcasted_iota(jnp.int32, shape, len(shape) - 1) < BLK
 
 
-def columns_to_rows(columns, first, count):
+def columns_to_row(columns, row_ref):
     rows = columns[0].shape[0]
     lane = lax.broadcasted_iota(jnp.int32, (rows, LANES), 1)
     table = jnp.zeros((rows, LANES), jnp.float32)
     for at, column in enumerate(columns):
-        table = jnp.where(lane == first + at, column, table)
-    return jnp.transpose(table)[:count]
+        table = jnp.where(lane == at, column, table)
+    table = jnp.transpose(table)
+    for at in range(len(columns)):
+        row_ref[:, at * rows:(at + 1) * rows] = table[at:at + 1]
 
 
 def teacher_kernel(owners, most, dev_ref, slot_ref, mentor_ref, weight_ref, out_ref, stats_ref, codes_ref, count_ref, place_ref):
     row_count, width = mentor_ref.shape
     half = row_count // 2
+    rows = half // CHUNKS
     topk = dev_ref.shape[0]
     tb_local = dev_ref.shape[1]
 
     for owner in range(owners):
         count_ref[owner] = 0
-    code_lane = lax.broadcasted_iota(jnp.int32, (8, LANES), 1)
+    code_lane = lax.broadcasted_iota(jnp.int32, (1, LANES), 1)
 
     def place(b, codes):
         for k in range(topk):
@@ -50,7 +55,7 @@
             codes = jnp.where(code_lane == position, slot_ref[k, b], codes)
         return codes
 
-    codes_ref[...] = lax.fori_loop(0, tb_local, place, jnp.full((8, LANES), -1, jnp.int32))
+    codes_ref[...] = lax.fori_loop(0, tb_local, place, jnp.full((1, LANES), -1, jnp.int32))
 
     tiles = width // LANES
     high = mentor_ref[:, :LANES]
@@ -78,7 +83,8 @@
         terms = jnp.dot(lhs, rhs, preferred_element_type=jnp.float32).astype(jnp.bfloat16)
         for at in range(2 * topk):
             term = terms[:, at * LANES:(at + 1) * LANES]
-            out_ref[place_ref[2 * topk * j + at]] = term
+            for chunk in range(CHUNKS):
+                out_ref[chunk, place_ref[2 * topk * j + at]] = term[chunk * rows:(chunk + 1) * rows]
             mass = mass + term.astype(jnp.float32)
         return total, mass
 
@@ -92,7 +98,7 @@
         jnp.sum(jnp.where(low, 0.0, mass), axis=1, keepdims=True),
     ], axis=0)
     total = jnp.sum(total, axis=1, keepdims=True)
-    stats_ref[...] = columns_to_rows([high, total, mass], 0, STATS)
+    columns_to_row([high, total, mass], stats_ref)
 
 
 def outer_partner(outer, far):
@@ -107,37 +113,37 @@
     dp, me = lax.axis_index("dp"), lax.axis_index("vocab")
     row_count, width = learner_ref.shape
     half = row_count // 2
+    rows = half // CHUNKS
     tiles = width // LANES
     slots = owners * most
     inner = owners // OUTER
     vocab_width = float(width * owners)
     low = low_lanes((half, LANES))
+    low_rows = low_lanes((rows, LANES))
 
     def partner(near, order):
         return outer_partner(me // inner, FAR[order]) * inner + lax.rem(lax.rem(me, inner) + near, inner)
 
     def copy_to(kind, near, order, src, dst):
-        peer = partner(near, order)
         slot = near * OUTER + order
         return pltpu.make_async_remote_copy(
-            src_ref=out_ref.at[peer] if src is None else src, dst_ref=dst.at[slot],
-            send_sem=send.at[kind, slot], recv_sem=recv.at[kind, slot],
-            device_id=(dp, peer), device_id_type=MESH)
-
-    def blocks(near, order):
-        return copy_to(0, near, order, None, received)
+            src_ref=src, dst_ref=dst.at[slot], send_sem=send.at[kind, slot], recv_sem=recv.at[kind, slot],
+            device_id=(dp, partner(near, order)), device_id_type=MESH)
+
+    def blocks(chunk, near, order):
+        return copy_to(chunk, near, order, out_ref.at[chunk, partner(near, order)], received.at[chunk])
 
     def teacher_stats(near, order):
-        return copy_to(1, near, order, stats_ref, teacher_table)
+        return copy_to(CHUNKS, near, order, stats_ref, teacher_table)
 
     def slot_codes(near, order):
-        return copy_to(2, near, order, codes_ref, code_table)
+        return copy_to(CHUNKS + 1, near, order, codes_ref, code_table)
 
     def student_stats(near, order):
-        return copy_to(3, near, order, message, student_table)
+        return copy_to(CHUNKS + 2, near, order, message, student_table)
 
     def losses(near, order):
-        return copy_to(4, near, order, loss_message, loss_table)
+        return copy_to(CHUNKS + 3, near, order, loss_message, loss_table)
 
     def each(action):
         for order in range(1, OUTER):
@@ -154,7 +160,7 @@
 
     def part_copy(k):
         return pltpu.make_async_remote_copy(
-            src_ref=part_loss, dst_ref=part_table.at[dp], send_sem=send.at[5, k], recv_sem=recv.at[5, k],
+            src_ref=part_loss, dst_ref=part_table.at[dp], send_sem=send.at[CHUNKS + 4, k], recv_sem=recv.at[CHUNKS + 4, k],
             device_id=(lax.rem(dp + k, parts), me), device_id_type=MESH)
 
     barrier = pltpu.get_barrier_semaphore()
@@ -168,14 +174,14 @@
     pl.semaphore_wait(barrier, owners + parts - 2)
 
     for order in range(1, OUTER):
-        blocks(0, order).start()
+        blocks(0, 0, order).start()
 
     def start_small(near, order):
         slot_codes(near, order).start()
         teacher_stats(near, order).start()
 
     each(start_small)
-    rest(lambda near, order: blocks(near, order).start())
+    rest(lambda near, order: blocks(0, near, order).start())
 
     teacher_table[0] = stats_ref[...]
     code_table[0] = codes_ref[...]
@@ -191,9 +197,11 @@
 
     total = lax.fori_loop(0, tiles, add_exp, jnp.zeros((row_count, LANES), jnp.float32))
     total = jnp.sum(total, axis=1, keepdims=True)
-    message[...] = columns_to_rows([high, total], 0, STATS)
+    columns_to_row([high, total], message)
     student_table[0] = message[...]
     each(lambda near, order: student_stats(near, order).start())
+    for chunk in range(1, CHUNKS):
+        each(lambda near, order: blocks(chunk, near, order).start())
 
     each(lambda near, order: slot_codes(near, order).wait())
     fetch = pltpu.make_async_copy(code_table, code_smem, local.at[0])
@@ -210,13 +218,15 @@
     history[pl.ds(slots, 1), :] = last
     fetch = pltpu.make_async_copy(history, history_smem, local.at[1])
     fetch.start()
-    sums[slots] = jnp.zeros((half, LANES), jnp.float32)
+    for chunk in range(CHUNKS):
+        sums[chunk, slots] = jnp.zeros((rows, LANES), jnp.float32)
 
     each(lambda near, order: teacher_stats(near, order).wait())
-    teacher_high = teacher_table[:, 0, :]
+    teacher_high, teacher_sum, teacher_mass = (
+        teacher_table[:, 0, at * row_count:(at + 1) * row_count] for at in range(TEACHER_STATS))
     teacher_scale = jnp.exp(teacher_high - jnp.max(teacher_high, axis=0, keepdims=True))
-    weight = teacher_scale / jnp.sum(teacher_table[:, 1, :] * teacher_scale, axis=0, keepdims=True)
-    target_total = jnp.sum(teacher_table[:, 2, :] * weight, axis=0, keepdims=True)
+    weight = teacher_scale / jnp.sum(teacher_sum * teacher_scale, axis=0, keepdims=True)
+    target_total = jnp.sum(teacher_mass * weight, axis=0, keepdims=True)
     fill = jnp.zeros((LANES - owners - 1, row_count), jnp.float32)
     columns = jnp.transpose(jnp.concatenate([weight, target_total, fill], axis=0))
     for source in range(owners):
@@ -225,52 +235,91 @@
     target_total = columns[:, owners:owners + 1] * vocab_width
     fetch.wait()
 
-    def add_blocks(slot, source_ref, index):
+    def add_blocks(chunk, slot, source_ref, index):
+        at_rows = pl.ds(chunk * rows, rows)
         for at in range(most):
             q = slot * most + at
             code = code_smem[slot, 0, me * most + at]
-            earlier = sums[history_smem[q, jnp.maximum(code, 0)]]
-            sums[q] = earlier + source_ref[index, at].astype(jnp.float32) * scale[slot]
-
-    add_blocks(0, out_ref, me)
-
-    def take(near, order):
-        blocks(near, order).wait()
-        slot = near * OUTER + order
-        add_blocks(slot, received, slot)
-
-    each(take)
-
-    each(lambda near, order: student_stats(near, order).wait())
-    student_high = student_table[:, 0, :]
-    top = jnp.max(student_high, axis=0, keepdims=True)
-    lse = top + jnp.log(jnp.sum(student_table[:, 1, :] * jnp.exp(student_high - top), axis=0, keepdims=True))
-    lse = jnp.transpose(jnp.concatenate([lse, jnp.zeros((LANES - 1, row_count), jnp.float32)], axis=0))[:, :1]
-
-    def pair(j, loss):
-        first = sums[history_smem[slots, 2 * j]]
-        second = sums[history_smem[slots, 2 * j + 1]]
+            earlier = sums[chunk, history_smem[q, jnp.maximum(code, 0)]]
+            sums[chunk, q] = earlier + source_ref[chunk, index, at].astype(jnp.float32) * scale[slot, at_rows, :]
+
+    def gather(chunk):
+        add_blocks(chunk, 0, out_ref, me)
+
+        def take(near, order):
+            blocks(chunk, near, order).wait()
+            slot = near * OUTER + order
+            add_blocks(chunk, slot, received, slot)
+
+        each(take)
+
+    def chunk_rows(chunk, column):
+        top = chunk * rows
+        return jnp.concatenate([column[top:top + rows], column[half + top:half + top + rows]], axis=0)
+
+    def tile(chunk, j):
+        first = sums[chunk, history_smem[slots, 2 * j]]
+        second = sums[chunk, history_smem[slots, 2 * j + 1]]
         target = jnp.concatenate([
-            jnp.where(low, first, pltpu.roll(second, BLK, 1)),
-            jnp.where(low, pltpu.roll(first, BLK, 1), second),
+            jnp.where(low_rows, first, pltpu.roll(second, BLK, 1)),
+            jnp.where(low_rows, pltpu.roll(first, BLK, 1), second),
         ], axis=0)
         at = pl.ds(pl.multiple_of(j * LANES, LANES), LANES)
-        logprob = learner_ref[:, at].astype(jnp.float32) / float(SMOOTHING_HEAT) - lse
-        grad_ref[:, at] = (target_total * jnp.exp(logprob) - vocab_width * target).astype(jnp.bfloat16)
-        return loss + jnp.where(target > 0.0, target * (jnp.log(target) - logprob), 0.0)
-
-    loss = lax.fori_loop(0, tiles, pair, jnp.zeros((row_count, LANES), jnp.float32))
-    loss = jnp.sum(loss.reshape(row_count // 8, 8, LANES), axis=0)
+        top = pl.ds(chunk * rows, rows)
+        bottom = pl.ds(half + chunk * rows, rows)
+        logits = jnp.concatenate([learner_ref[top, at], learner_ref[bottom, at]], axis=0).astype(jnp.float32)
+        return target, logits / float(SMOOTHING_HEAT), at, top, bottom
+
+    def add_loss(chunk, loss):
+        lse_rows = chunk_rows(chunk, lse)
+
+        def body(j, loss):
+            target, logits, _, _, _ = tile(chunk, j)
+            return loss + jnp.where(target > 0.0, target * (jnp.log(target) - (logits - lse_rows)), 0.0)
+
+        return lax.fori_loop(0, tiles, body, loss)
+
+    def write_gradient(chunk, first, end):
+        lse_rows, total_rows = chunk_rows(chunk, lse), chunk_rows(chunk, target_total)
+
+        def body(j, carry):
+            target, logits, at, top, bottom = tile(chunk, j)
+            grad = (total_rows * jnp.exp(logits - lse_rows) - vocab_width * target).astype(jnp.bfloat16)
+            grad_ref[top, at] = grad[:rows]
+            grad_ref[bottom, at] = grad[rows:]
+            return carry
+
+        lax.fori_loop(first, end, body, 0)
+
+    gather(0)
+    each(lambda near, order: student_stats(near, order).wait())
+    student_high, student_sum = (
+        student_table[:, 0, at * row_count:(at + 1) * row_count] for at in range(STUDENT_STATS))
+    top = jnp.max(student_high, axis=0, keepdims=True)
+    lse = top + jnp.log(jnp.sum(student_sum * jnp.exp(student_high - top), axis=0, keepdims=True))
+    lse = jnp.transpose(jnp.concatenate([lse, jnp.zeros((LANES - 1, row_count), jnp.float32)], axis=0))[:, :1]
+
+    loss = jnp.zeros((2 * rows, LANES), jnp.float32)
+    for chunk in range(CHUNKS):
+        if chunk:
+            gather(chunk)
+        loss = add_loss(chunk, loss)
+        if chunk < CHUNKS - 1:
+            write_gradient(chunk, 0, tiles)
+
+    loss = jnp.sum(loss.reshape(2 * rows // 8, 8, LANES), axis=0)
     part_loss[...] = loss
     for k in range(1, parts):
         part_copy(k).start()
     part_table[dp] = loss
+    write_gradient(CHUNKS - 1, 0, tiles // 2)
     for k in range(1, parts):
         part_copy(k).wait()
     loss = jnp.sum(part_table[...], axis=0)
     loss_message[...] = loss
     each(lambda near, order: losses(near, order).start())
     loss_table[0] = loss
+    write_gradient(CHUNKS - 1, tiles // 2, tiles)
     each(lambda near, order: losses(near, order).wait())
     totals = jnp.sum(jnp.sum(loss_table[...], axis=1), axis=1, keepdims=True)
     loss_ref[...] = jnp.sum(totals, axis=0, keepdims=True) * loss_scale
@@ -279,7 +328,7 @@
 def per_device(mentor_score_matrix, learner_score_matrix, align_dev, align_slot, align_weight):
     parts, owners = lax.axis_size("dp"), lax.axis_size("vocab")
     row_count, _ = mentor_score_matrix.shape
-    half = row_count // 2
+    rows = row_count // (2 * CHUNKS)
     tb_local, topk = align_dev.shape
     most = max(2, 3 * tb_local * topk // (2 * owners))
     width = learner_score_matrix.shape[1]
@@ -292,9 +341,9 @@
     outgoing, stats, codes = pl.pallas_call(
         functools.partial(teacher_kernel, owners, most),
         out_shape=(
-            jax.ShapeDtypeStruct((owners * most, half, LANES), jnp.bfloat16),
-            jax.ShapeDtypeStruct((STATS, row_count), jnp.float32),
-            jax.ShapeDtypeStruct((8, LANES), jnp.int32),
+            jax.ShapeDtypeStruct((CHUNKS, owners * most, rows, LANES), jnp.bfloat16),
+            jax.ShapeDtypeStruct((1, TEACHER_STATS * row_count), jnp.float32),
+            jax.ShapeDtypeStruct((1, LANES), jnp.int32),
         ),
         in_specs=[smem, smem, vmem, vmem],
         out_specs=(vmem, vmem, vmem),
@@ -316,28 +365,28 @@
         in_specs=[vmem, vmem, vmem, vmem],
         out_specs=(vmem, vmem),
         scratch_shapes=[
-            pltpu.VMEM((owners, most, half, LANES), jnp.bfloat16),
-            pltpu.VMEM((slots + 1, half, LANES), jnp.float32),
-            pltpu.VMEM((owners, half, LANES), jnp.float32),
-            pltpu.VMEM((STATS, row_count), jnp.float32),
-            pltpu.VMEM((owners, STATS, row_count), jnp.float32),
-            pltpu.VMEM((owners, STATS, row_count), jnp.float32),
-            pltpu.VMEM((owners, 8, LANES), jnp.int32),
-            pltpu.SMEM((owners, 8, LANES), jnp.int32),
+            pltpu.VMEM((CHUNKS, owners, most, rows, LANES), jnp.bfloat16),
+            pltpu.VMEM((CHUNKS, slots + 1, rows, LANES), jnp.float32),
+            pltpu.VMEM((owners, CHUNKS * rows, LANES), jnp.float32),
+            pltpu.VMEM((1, STUDENT_STATS * row_count), jnp.float32),
+            pltpu.VMEM((owners, 1, TEACHER_STATS * row_count), jnp.float32),
+            pltpu.VMEM((owners, 1, STUDENT_STATS * row_count), jnp.float32),
+            pltpu.VMEM((owners, 1, LANES), jnp.int32),
+            pltpu.SMEM((owners, 1, LANES), jnp.int32),
             pltpu.VMEM((history_rows, LANES), jnp.int32),
             pltpu.SMEM((history_rows, LANES), jnp.int32),
             small,
             pltpu.VMEM((parts, 8, LANES), jnp.float32),
             small,
             pltpu.VMEM((owners, 8, LANES), jnp.float32),
-            pltpu.SemaphoreType.DMA((6, owners)),
-            pltpu.SemaphoreType.DMA((6, owners)),
+            pltpu.SemaphoreType.DMA((CHUNKS + 5, owners)),
+            pltpu.SemaphoreType.DMA((CHUNKS + 5, owners)),
             pltpu.SemaphoreType.DMA((2,)),
         ],
         compiler_params=pltpu.CompilerParams(
             collective_id=0, has_side_effects=True, vmem_limit_bytes=VMEM_BYTES),
         name="exchange_and_gradient",
-    )(outgoing.reshape(owners, most, half, LANES), stats, codes, learner_score_matrix)
+    )(outgoing.reshape(CHUNKS, owners, most, rows, LANES), stats, codes, learner_score_matrix)
     return scaled_grad, loss[0, 0]
 
 

time: 99 us -> 90.8 us (0.917)
  Pallas kernels: 92.2 us -> 84 us
    pallas_call x1, Pallas kernels: 87.6 us -> 79.5 us  [per_device(): pl.pallas_call(functools.partial(student_kernel, parts, owners, most, los...]
where the time goes in v4:
time: 90.8 us; the launch traced here: 90.6 us
  Pallas kernels  84 us (93%)
  local copies, waits for them, and re-layouts  3.64 us (4%)
  between operations  2.4 us (3%)
    pallas_call x1, Pallas kernels, per_device(): pl.pallas_call(functools.partial(student_kernel, parts, owners, most, los...  79.5 us
    pallas_call x1, Pallas kernels, per_device(): pl.pallas_call(functools.partial(teacher_kernel, owners, most), out_shape...  4.56 us
    reshape x1, local copies, waits for them, and re-layouts, per_device(): weight = align_weight.reshape(tb_local * topk, BLK, BLK)  2.3 us

profile of v4, /device:TPU:0, one launch (start us, length us, event | category | flops | bytes accessed | tf_op | source)
XLA Modules:
  0.0 90.6 jit_solution(1336036634018191328)
XLA Ops:
  0.6 0.0 copy-start.3
  0.6 0.0 copy-start.2
  0.6 0.0 copy-start.1
  0.7 2.3 %reshape.10 = bf16[60,64,64]{2,1,0:T(8,128)(2,1)S(1)} reshape(bf16[30,2,4096]{2,1,0:T(2,128)(2,1)} %param.9) | data formatting | bytes 983040 | tf_op jit(solution)/shard_map/reshape | solution.py:338
  3.0 0.0 copy-start
  3.0 0.5 pad_maximum_fusion.weight_ref
  3.5 0.0 copy-done.3
  3.5 0.0 copy-done.2
  3.6 0.0 copy-done.1
  3.6 4.6 %teacher_terms.1 = (bf16[2,80,64,128]{3,2,1,0:T(8,128)(2,1)S(1)}, f32[1,768]{1,0:T(1,128)S(1)}, s32[1,128]{1,0:T(1,128)S(1)}) custom-call(s32[2,30]{1,0:T(2,128)S(1)} %bitcast.5, s32[2,30]{1,0:T(2,128)S(1)} %bitcast.6, bf16[256,1920]{1,0:T(8,128)(2,1)S(1)} %copy-done.1, bf16[60,64,128]{2,1,0:T(8,128)(2,1)S(1)} %pad_maximum_fusion.weight_ref), custom_call_target="tpu_custom_call" | custom-call | tf_op jit(solution)/shard_map/teacher_terms/pallas_call | solution.py:341
  8.1 0.0 copy-done
  8.1 79.5 %exchange_and_gradient.1 = (bf16[256,4096]{1,0:T(8,128)(2,1)S(1)}, f32[1,1]{1,0:T(1,128)}) custom-call(bf16[2,16,5,64,128]{4,3,2,1,0:T(8,128)(2,1)S(1)} %bitcast.4, f32[1,768]{1,0:T(1,128)S(1)} %get-tuple-element.8.stats_ref, s32[1,128]{1,0:T(1,128)S(1)} %get-tuple-element.9.codes_ref, bf16[256,4096]{1,0:T(8,128)(2,1)S(1)} %copy-done), custom_call_target="tpu_custom_call" | custom-call | tf_op jit(solution)/shard_map/exchange_and_gradient/pallas_call | solution.py:359
  87.6 1.3 %copy.9 = bf16[256,4096]{1,0:T(8,128)(2,1)} copy(bf16[256,4096]{1,0:T(8,128)(2,1)S(1)} %get-tuple-element.14) | data formatting | bytes 4194304
Async XLA Ops:
  0.6 2.9 %copy-start.3 = (s32[30,2]{0,1:T(2,128)S(1)}, s32[30,2]{0,1:T(2,128)}, u32[]{:S(2)}) copy-start(s32[30,2]{0,1:T(2,128)} %param.8) | copy-start | bytes 724
  0.6 2.9 %copy-start.2 = (s32[30,2]{0,1:T(2,128)S(1)}, s32[30,2]{0,1:T(2,128)}, u32[]{:S(2)}) copy-start(s32[30,2]{0,1:T(2,128)} %param.7) | copy-start | bytes 724
  0.6 2.9 %copy-start.1 = (bf16[256,1920]{1,0:T(8,128)(2,1)S(1)}, bf16[256,1920]{1,0:T(8,128)(2,1)}, u32[]{:S(2)}) copy-start(bf16[256,1920]{1,0:T(8,128)(2,1)} %mentor_ref.1) | copy-start | bytes 2949124
  3.0 5.2 %copy-start = (bf16[256,4096]{1,0:T(8,128)(2,1)S(1)}, bf16[256,4096]{1,0:T(8,128)(2,1)}, u32[]{:S(2)}) copy-start(bf16[256,4096]{1,0:T(8,128)(2,1)} %learner_ref.1) | copy-start | bytes 6291460

commit v5 on v4

--- a/solution.py
+++ b/solution.py
@@ -34,79 +34,13 @@
         row_ref[:, at * rows:(at + 1) * rows] = table[at:at + 1]
 
 
-def teacher_kernel(owners, most, dev_ref, slot_ref, mentor_ref, weight_ref, out_ref, stats_ref, codes_ref, count_ref, place_ref):
-    row_count, width = mentor_ref.shape
-    half = row_count // 2
-    rows = half // CHUNKS
-    topk = dev_ref.shape[0]
-    tb_local = dev_ref.shape[1]
-
-    for owner in range(owners):
-        count_ref[owner] = 0
-    code_lane = lax.broadcasted_iota(jnp.int32, (1, LANES), 1)
-
-    def place(b, codes):
-        for k in range(topk):
-            owner = dev_ref[k, b]
-            earlier = count_ref[owner]
-            count_ref[owner] = earlier + 1
-            position = owner * most + earlier
-            place_ref[b * topk + k] = position
-            codes = jnp.where(code_lane == position, slot_ref[k, b], codes)
-        return codes
-
-    codes_ref[...] = lax.fori_loop(0, tb_local, place, jnp.full((1, LANES), -1, jnp.int32))
-
-    tiles = width // LANES
-    high = mentor_ref[:, :LANES]
-    for tile in range(1, tiles):
-        high = jnp.maximum(high, mentor_ref[:, tile * LANES:(tile + 1) * LANES])
-    high = jnp.max(high.astype(jnp.float32), axis=1, keepdims=True) / float(SMOOTHING_HEAT)
-
-    low = low_lanes((BLK, LANES))
-    none = jnp.zeros((BLK, LANES), jnp.bfloat16)
-
-    def pair(j, carry):
-        total, mass = carry
-        x = mentor_ref[:, pl.ds(pl.multiple_of(j * LANES, LANES), LANES)].astype(jnp.float32)
-        e = jnp.exp(x / float(SMOOTHING_HEAT) - high)
-        total = total + e
-        e = e.astype(jnp.bfloat16)
-        lhs = jnp.concatenate([e[:half], e[half:]], axis=1)
-        lefts, rights = [], []
-        for b in range(2):
-            blocks = [weight_ref[(2 * j + b) * topk + k] for k in range(topk)]
-            pad_before, pad_after = [none] * (topk * b), [none] * (topk * (1 - b))
-            lefts.append(jnp.concatenate(pad_before + [jnp.where(low, w, none) for w in blocks] + pad_after, axis=1))
-            rights.append(jnp.concatenate(pad_before + [jnp.where(low, none, w) for w in blocks] + pad_after, axis=1))
-        rhs = jnp.concatenate(lefts + rights, axis=0)
-        terms = jnp.dot(lhs, rhs, preferred_element_type=jnp.float32).astype(jnp.bfloat16)
-        for at in range(2 * topk):
-            term = terms[:, at * LANES:(at + 1) * LANES]
-            for chunk in range(CHUNKS):
-                out_ref[chunk, place_ref[2 * topk * j + at]] = term[chunk * rows:(chunk + 1) * rows]
-            mass = mass + term.astype(jnp.float32)
-        return total, mass
-
-    total, mass = lax.fori_loop(
-        0, tiles, pair,
-        (jnp.zeros((row_count, LANES), jnp.float32), jnp.zeros((half, LANES), jnp.float32)),
-    )
-    low = low_lanes((half, LANES))
-    mass = jnp.concatenate([
-        jnp.sum(jnp.where(low, mass, 0.0), axis=1, keepdims=True),
-        jnp.sum(jnp.where(low, 0.0, mass), axis=1, keepdims=True),
-    ], axis=0)
-    total = jnp.sum(total, axis=1, keepdims=True)
-    columns_to_row([high, total, mass], stats_ref)
-
-
 def outer_partner(outer, far):
     return (outer, outer + 1 - 2 * lax.rem(outer, 2), lax.rem(outer + 2, OUTER), OUTER - 1 - outer)[far]
 
 
 def student_kernel(parts, owners, most, loss_scale,
-                   out_ref, stats_ref, codes_ref, learner_ref, grad_ref, loss_ref,
+                   dev_ref, slot_ref, mentor_ref, weight_ref, learner_ref, grad_ref, loss_ref,
+                   exps, masks, mass, edges, edges_smem, own_codes, own_codes_smem, out, stats,
                    received, sums, scale, message, teacher_table, student_table, code_table, code_smem,
                    history, history_smem, part_loss, part_table, loss_message, loss_table,
                    send, recv, local):
@@ -131,13 +65,13 @@
             device_id=(dp, partner(near, order)), device_id_type=MESH)
 
     def blocks(chunk, near, order):
-        return copy_to(chunk, near, order, out_ref.at[chunk, partner(near, order)], received.at[chunk])
+        return copy_to(chunk, near, order, out.at[chunk, near * OUTER + order], received.at[chunk])
 
     def teacher_stats(near, order):
-        return copy_to(CHUNKS, near, order, stats_ref, teacher_table)
+        return copy_to(CHUNKS, near, order, stats, teacher_table)
 
     def slot_codes(near, order):
-        return copy_to(CHUNKS + 1, near, order, codes_ref, code_table)
+        return copy_to(CHUNKS + 1, near, order, own_codes, code_table)
 
     def student_stats(near, order):
         return copy_to(CHUNKS + 2, near, order, message, student_table)
@@ -171,20 +105,92 @@
     each(greet)
     for k in range(1, parts):
         pl.semaphore_signal(barrier, inc=1, device_id=(lax.rem(dp + k, parts), me), device_id_type=MESH)
+
+    topk, tb_local = dev_ref.shape
+    lane = lax.broadcasted_iota(jnp.int32, (1, LANES), 1)
+    slot_owner = jnp.zeros((1, LANES), jnp.int32)
+    for owner in range(1, owners + 1):
+        slot_owner = slot_owner + jnp.where(lane >= owner * most, 1, 0)
+    slot_place = lane - slot_owner * most
+
+    def route(b, carry):
+        count, edge_of, codes = carry
+        for k in range(topk):
+            hit = slot_owner == dev_ref[k, b]
+            here = jnp.logical_and(hit, count == slot_place)
+            edge_of = jnp.where(here, b * topk + k, edge_of)
+            codes = jnp.where(here, slot_ref[k, b], codes)
+            count = count + jnp.where(hit, 1, 0)
+        return count, edge_of, codes
+
+    none = jnp.zeros((1, LANES), jnp.int32)
+    _, edge_of, codes = lax.fori_loop(0, tb_local, route, (none, none, none - 1))
+    edges[...] = edge_of
+    own_codes[...] = codes
+    fetches = [pltpu.make_async_copy(edges, edges_smem, local.at[2]),
+               pltpu.make_async_copy(own_codes, own_codes_smem, local.at[3])]
+    for fetch in fetches:
+        fetch.start()
+
+    row = lax.broadcasted_iota(jnp.int32, (2 * LANES, LANES), 0)
+    side = lax.broadcasted_iota(jnp.int32, (2 * LANES, LANES), 1) >= BLK
+    for parity in range(2):
+        low_part = jnp.logical_and(row >= parity * BLK, row < (parity + 1) * BLK)
+        high_part = jnp.logical_and(row >= LANES + parity * BLK, row < LANES + (parity + 1) * BLK)
+        kept = jnp.where(side, jnp.where(high_part, 1.0, 0.0), jnp.where(low_part, 1.0, 0.0))
+        masks[parity] = kept.astype(jnp.bfloat16)
+
+    pairs = mentor_ref.shape[1] // LANES
+    high = mentor_ref[:, :LANES]
+    for pair in range(1, pairs):
+        high = jnp.maximum(high, mentor_ref[:, pair * LANES:(pair + 1) * LANES])
+    teacher_high = jnp.max(high.astype(jnp.float32), axis=1, keepdims=True) / float(SMOOTHING_HEAT)
+
+    def exp_pair(j, total):
+        x = mentor_ref[:, pl.ds(pl.multiple_of(j * LANES, LANES), LANES)].astype(jnp.float32)
+        e = jnp.exp(x / float(SMOOTHING_HEAT) - teacher_high)
+        rounded = e.astype(jnp.bfloat16)
+        exps[j] = jnp.concatenate([rounded[:half], rounded[half:]], axis=1)
+        return total + e
+
+    teacher_sum = lax.fori_loop(0, pairs, exp_pair, jnp.zeros((row_count, LANES), jnp.float32))
+    mass[...] = jnp.zeros((half, LANES), jnp.float32)
+    for fetch in fetches:
+        fetch.wait()
+
+    def fill_slots(near, order):
+        peer = partner(near, order)
+        for at in range(most):
+            edge = edges_smem[0, peer * most + at]
+            weight = weight_ref[edge]
+            rhs = jnp.concatenate([weight] * 4, axis=0) * masks[lax.rem(edge // topk, 2)]
+            term = jnp.dot(exps[edge // (2 * topk)], rhs, preferred_element_type=jnp.float32).astype(jnp.bfloat16)
+            for chunk in range(CHUNKS):
+                out[chunk, near * OUTER + order, at] = term[chunk * rows:(chunk + 1) * rows]
+            used = jnp.where(own_codes_smem[0, peer * most + at] >= 0, 1.0, 0.0)
+            mass[...] = mass[...] + term.astype(jnp.float32) * used
+
     pl.semaphore_wait(barrier, owners + parts - 2)
 
+    def send_first(near, order):
+        fill_slots(near, order)
+        blocks(0, near, order).start()
+
     for order in range(1, OUTER):
-        blocks(0, 0, order).start()
-
-    def start_small(near, order):
-        slot_codes(near, order).start()
-        teacher_stats(near, order).start()
-
-    each(start_small)
-    rest(lambda near, order: blocks(0, near, order).start())
-
-    teacher_table[0] = stats_ref[...]
-    code_table[0] = codes_ref[...]
+        send_first(0, order)
+    each(lambda near, order: slot_codes(near, order).start())
+    rest(send_first)
+    fill_slots(0, 0)
+    filled = mass[...]
+    target_mass = jnp.concatenate([
+        jnp.sum(jnp.where(low, filled, 0.0), axis=1, keepdims=True),
+        jnp.sum(jnp.where(low, 0.0, filled), axis=1, keepdims=True),
+    ], axis=0)
+    columns_to_row([teacher_high, jnp.sum(teacher_sum, axis=1, keepdims=True), target_mass], stats)
+    each(lambda near, order: teacher_stats(near, order).start())
+
+    teacher_table[0] = stats[...]
+    code_table[0] = own_codes[...]
 
     def tile_of(j):
         return learner_ref[:, pl.ds(pl.multiple_of(j * LANES, LANES), LANES)]
@@ -207,7 +213,6 @@
     fetch = pltpu.make_async_copy(code_table, code_smem, local.at[0])
     fetch.start()
     fetch.wait()
-    lane = lax.broadcasted_iota(jnp.int32, (1, LANES), 1)
 
     def note(q, last):
         history[pl.ds(q, 1), :] = last
@@ -244,7 +249,7 @@
             sums[chunk, q] = earlier + source_ref[chunk, index, at].astype(jnp.float32) * scale[slot, at_rows, :]
 
     def gather(chunk):
-        add_blocks(chunk, 0, out_ref, me)
+        add_blocks(chunk, 0, out, 0)
 
         def take(near, order):
             blocks(chunk, near, order).wait()
@@ -338,20 +343,6 @@
     weight = align_weight.reshape(tb_local * topk, BLK, BLK)
     weight = jnp.concatenate([weight, weight], axis=2)
 
-    outgoing, stats, codes = pl.pallas_call(
-        functools.partial(teacher_kernel, owners, most),
-        out_shape=(
-            jax.ShapeDtypeStruct((CHUNKS, owners * most, rows, LANES), jnp.bfloat16),
-            jax.ShapeDtypeStruct((1, TEACHER_STATS * row_count), jnp.float32),
-            jax.ShapeDtypeStruct((1, LANES), jnp.int32),
-        ),
-        in_specs=[smem, smem, vmem, vmem],
-        out_specs=(vmem, vmem, vmem),
-        scratch_shapes=[pltpu.SMEM((owners,), jnp.int32), pltpu.SMEM((tb_local * topk,), jnp.int32)],
-        compiler_params=pltpu.CompilerParams(vmem_limit_bytes=VMEM_BYTES),
-        name="teacher_terms",
-    )(align_dev.T, align_slot.T, mentor_score_matrix, weight)
-
     loss_scale = float(SMOOTHING_HEAT) * float(SMOOTHING_HEAT) / float(row_count * parts)
     slots = owners * most
     history_rows = (slots // 8 + 1) * 8
@@ -362,9 +353,18 @@
             jax.ShapeDtypeStruct((row_count, width), jnp.bfloat16),
             jax.ShapeDtypeStruct((1, 1), jnp.float32),
         ),
-        in_specs=[vmem, vmem, vmem, vmem],
+        in_specs=[smem, smem, vmem, vmem, vmem],
         out_specs=(vmem, vmem),
         scratch_shapes=[
+            pltpu.VMEM((mentor_score_matrix.shape[1] // LANES, CHUNKS * rows, 2 * LANES), jnp.bfloat16),
+            pltpu.VMEM((2, 2 * LANES, LANES), jnp.bfloat16),
+            pltpu.VMEM((CHUNKS * rows, LANES), jnp.float32),
+            pltpu.VMEM((1, LANES), jnp.int32),
+            pltpu.SMEM((1, LANES), jnp.int32),
+            pltpu.VMEM((1, LANES), jnp.int32),
+            pltpu.SMEM((1, LANES), jnp.int32),
+            pltpu.VMEM((CHUNKS, owners, most, rows, LANES), jnp.bfloat16),
+            pltpu.VMEM((1, TEACHER_STATS * row_count), jnp.float32),
             pltpu.VMEM((CHUNKS, owners, most, rows, LANES), jnp.bfloat16),
             pltpu.VMEM((CHUNKS, slots + 1, rows, LANES), jnp.float32),
             pltpu.VMEM((owners, CHUNKS * rows, LANES), jnp.float32),
@@ -381,12 +381,12 @@
             pltpu.VMEM((owners, 8, LANES), jnp.float32),
             pltpu.SemaphoreType.DMA((CHUNKS + 5, owners)),
             pltpu.SemaphoreType.DMA((CHUNKS + 5, owners)),
-            pltpu.SemaphoreType.DMA((2,)),
+            pltpu.SemaphoreType.DMA((4,)),
         ],
         compiler_params=pltpu.CompilerParams(
             collective_id=0, has_side_effects=True, vmem_limit_bytes=VMEM_BYTES),
-        name="exchange_and_gradient",
-    )(outgoing.reshape(CHUNKS, owners, most, rows, LANES), stats, codes, learner_score_matrix)
+        name="distillation",
+    )(align_dev.T, align_slot.T, mentor_score_matrix, weight, learner_score_matrix)
     return scaled_grad, loss[0, 0]
 
 

time: 90.8 us -> 89.4 us (0.985)
  Pallas kernels: 84 us -> 80.3 us
  other arithmetic: 0.54 us -> 2.04 us
    pallas_call x1 -> x0, Pallas kernels: 4.56 us -> none  [per_device(): pl.pallas_call(functools.partial(teacher_kernel, owners, most), out_shape...]
    concatenate x1, other arithmetic: 0.54 us -> 2.04 us  [per_device(): weight = jnp.concatenate([weight, weight], axis=2)]
where the time goes in v5:
time: 89.4 us; the launch traced here: 89.2 us
  Pallas kernels  80.3 us (90%)
  local copies, waits for them, and re-layouts  4.42 us (5%)
  between operations  2.45 us (3%)
  other arithmetic  2.04 us (2%)
    pallas_call x1, Pallas kernels, per_device(): pl.pallas_call(functools.partial(student_kernel, parts, owners, most, los...  80.3 us
    reshape x1, local copies, waits for them, and re-layouts, per_device(): weight = align_weight.reshape(tb_local * topk, BLK, BLK)  3.08 us
    concatenate x1, other arithmetic, per_device(): weight = jnp.concatenate([weight, weight], axis=2)  2.04 us

profile of v5, /device:TPU:0, one launch (start us, length us, event | category | flops | bytes accessed | tf_op | source)
XLA Modules:
  0.0 89.2 jit_solution(16590063295652373566)
XLA Ops:
  0.6 0.0 copy-start.3
  0.6 0.0 copy-start.2
  0.7 0.0 copy-start
  0.7 0.0 copy-start.1
  0.7 3.1 %reshape.7 = bf16[60,64,64]{2,1,0:T(8,128)(2,1)} reshape(bf16[30,2,4096]{2,1,0:T(2,128)(2,1)} %param.9) | data formatting | bytes 983040 | tf_op jit(solution)/shard_map/reshape | solution.py:343
  3.8 2.0 %pad_maximum_fusion.weight_ref = bf16[60,64,128]{2,1,0:T(8,128)(2,1)S(1)} fusion(bf16[60,64,64]{2,1,0:T(8,128)(2,1)} %reshape.7), kind=kLoop, calls=%fused_computation | loop fusion | flops 1966080 | bytes 1474560 | tf_op jit(solution)/shard_map/concatenate | solution.py:344
  5.8 0.0 copy-done.3
  5.8 0.0 copy-done.2
  5.8 0.0 copy-done
  5.8 0.0 copy-done.1
  5.8 80.3 %distillation.1 = (bf16[256,4096]{1,0:T(8,128)(2,1)S(1)}, f32[1,1]{1,0:T(1,128)}) custom-call(s32[2,30]{1,0:T(2,128)S(1)} %bitcast.3, s32[2,30]{1,0:T(2,128)S(1)} %bitcast.4, bf16[256,1920]{1,0:T(8,128)(2,1)S(1)} %copy-done.1, bf16[60,64,128]{2,1,0:T(8,128)(2,1)S(1)} %pad_maximum_fusion.weight_ref, bf16[256,4096]{1,0:T(8,128)(2,1)S(1)} %copy-done), custom_call_target="tpu_custom_call" | custom-call | tf_op jit(solution)/shard_map/distillation/pallas_call | solution.py:350
  86.2 1.3 %copy.9 = bf16[256,4096]{1,0:T(8,128)(2,1)} copy(bf16[256,4096]{1,0:T(8,128)(2,1)S(1)} %get-tuple-element.8) | data formatting | bytes 4194304
Async XLA Ops:
  0.6 5.2 %copy-start.3 = (s32[30,2]{0,1:T(2,128)S(1)}, s32[30,2]{0,1:T(2,128)}, u32[]{:S(2)}) copy-start(s32[30,2]{0,1:T(2,128)} %param.8) | copy-start | bytes 724
  0.6 5.2 %copy-start.2 = (s32[30,2]{0,1:T(2,128)S(1)}, s32[30,2]{0,1:T(2,128)}, u32[]{:S(2)}) copy-start(s32[30,2]{0,1:T(2,128)} %param.7) | copy-start | bytes 724
  0.7 5.2 %copy-start = (bf16[256,4096]{1,0:T(8,128)(2,1)S(1)}, bf16[256,4096]{1,0:T(8,128)(2,1)}, u32[]{:S(2)}) copy-start(bf16[256,4096]{1,0:T(8,128)(2,1)} %learner_ref.1) | copy-start | bytes 6291460
  0.7 5.2 %copy-start.1 = (bf16[256,1920]{1,0:T(8,128)(2,1)S(1)}, bf16[256,1920]{1,0:T(8,128)(2,1)}, u32[]{:S(2)}) copy-start(bf16[256,1920]{1,0:T(8,128)(2,1)} %mentor_ref.1) | copy-start | bytes 2949124

commit v6 on v5

--- a/solution.py
+++ b/solution.py
@@ -162,7 +162,7 @@
         peer = partner(near, order)
         for at in range(most):
             edge = edges_smem[0, peer * most + at]
-            weight = weight_ref[edge]
+            weight = jnp.concatenate([weight_ref[edge]] * 2, axis=1)
             rhs = jnp.concatenate([weight] * 4, axis=0) * masks[lax.rem(edge // topk, 2)]
             term = jnp.dot(exps[edge // (2 * topk)], rhs, preferred_element_type=jnp.float32).astype(jnp.bfloat16)
             for chunk in range(CHUNKS):
@@ -341,7 +341,6 @@
     smem = pl.BlockSpec(memory_space=pltpu.SMEM)
 
     weight = align_weight.reshape(tb_local * topk, BLK, BLK)
-    weight = jnp.concatenate([weight, weight], axis=2)
 
     loss_scale = float(SMOOTHING_HEAT) * float(SMOOTHING_HEAT) / float(row_count * parts)
     slots = owners * most

time: 89.4 us -> 89.6 us (level)
  local copies, waits for them, and re-layouts: 4.42 us -> 6.57 us
  other arithmetic: 2.04 us -> 0 us
    unnamed x9, local copies, waits for them, and re-layouts: 1.34 us -> 4.27 us
    concatenate x1 -> x0, other arithmetic: 2.04 us -> none  [per_device(): weight = jnp.concatenate([weight, weight], axis=2)]
where the time goes in v6:
time: 89.6 us; the launch traced here: 89.3 us
  Pallas kernels  80.4 us (90%)
  local copies, waits for them, and re-layouts  6.57 us (7%)
  between operations  2.42 us (3%)
    pallas_call x1, Pallas kernels, per_device(): pl.pallas_call(functools.partial(student_kernel, parts, owners, most, los...  80.4 us
    unnamed x9, local copies, waits for them, and re-layouts  4.27 us
    reshape x1, local copies, waits for them, and re-layouts, per_device(): weight = align_weight.reshape(tb_local * topk, BLK, BLK)  2.3 us

profile of v6, /device:TPU:0, one launch (start us, length us, event | category | flops | bytes accessed | tf_op | source)
XLA Modules:
  0.0 89.3 jit_solution(9963823214723550995)
XLA Ops:
  0.6 0.0 copy-start.1
  0.6 2.3 %reshape.7.weight_ref = bf16[60,64,64]{2,1,0:T(8,128)(2,1)S(1)} reshape(bf16[30,2,4096]{2,1,0:T(2,128)(2,1)} %param.9) | data formatting | bytes 983040 | tf_op jit(solution)/shard_map/reshape | solution.py:343
  2.9 0.0 copy-done.1
  3.0 0.0 copy-start
  3.0 1.6 %copy-done = bf16[256,4096]{1,0:T(8,128)(2,1)S(1)} copy-done((bf16[256,4096]{1,0:T(8,128)(2,1)S(1)}, bf16[256,4096]{1,0:T(8,128)(2,1)}, u32[]{:S(2)}) %copy-start) | copy-done | bytes 2097176
  4.6 0.0 copy-start.2
  4.6 0.7 copy-done.2
  5.2 0.0 copy-start.3
  5.2 0.7 copy-done.3
  5.9 80.4 %distillation.1 = (bf16[256,4096]{1,0:T(8,128)(2,1)S(1)}, f32[1,1]{1,0:T(1,128)}) custom-call(s32[2,30]{1,0:T(2,128)S(1)} %bitcast.3, s32[2,30]{1,0:T(2,128)S(1)} %bitcast.4, bf16[256,1920]{1,0:T(8,128)(2,1)S(1)} %copy-done.1, bf16[60,64,64]{2,1,0:T(8,128)(2,1)S(1)} %reshape.7.weight_ref, bf16[256,4096]{1,0:T(8,128)(2,1)S(1)} %copy-done), custom_call_target="tpu_custom_call" | custom-call | tf_op jit(solution)/shard_map/distillation/pallas_call | solution.py:349
  86.3 1.3 %copy.9 = bf16[256,4096]{1,0:T(8,128)(2,1)} copy(bf16[256,4096]{1,0:T(8,128)(2,1)S(1)} %get-tuple-element.8) | data formatting | bytes 4194304
Async XLA Ops:
  0.6 2.3 %copy-start.1 = (bf16[256,1920]{1,0:T(8,128)(2,1)S(1)}, bf16[256,1920]{1,0:T(8,128)(2,1)}, u32[]{:S(2)}) copy-start(bf16[256,1920]{1,0:T(8,128)(2,1)} %mentor_ref.1) | copy-start | bytes 2949124
  3.0 1.6 %copy-start = (bf16[256,4096]{1,0:T(8,128)(2,1)S(1)}, bf16[256,4096]{1,0:T(8,128)(2,1)}, u32[]{:S(2)}) copy-start(bf16[256,4096]{1,0:T(8,128)(2,1)} %learner_ref.1) | copy-start | bytes 6291460
  4.6 0.7 copy-start.2
  5.2 0.7 copy-start.3
